TPU v7x, 32 devices: a whole 2x2x4 slice. The times are simulated.
32 devices in a mesh: rows: 8 (over z, y), hid: 4 (over x, core).
Axes of the slice: x: 2, y: 2, z: 4, core: 2. Of those that a mesh axis runs over, the one named last changes fastest.
Arguments:
- grid_input: bfloat16 [131072, 78], P('rows'), may hold values from -6 to 6
- grid_target: bfloat16 [131072, 78], P('rows'), may hold values from -6 to 6
- live_points: int32 [8], P('rows'), may hold values from 5461 to 16384, as said below
- level_weight: int32 [78], replicated, may hold values from 1 to 10
- g2m_index: int32 [16384, 8], P('rows'), may hold values from 0 to 16383
- m2m_index: int32 [16384, 6], P('rows'), may hold values from 0 to 2047
- m2g_index: int32 [131072, 3], P('rows'), may hold values from 0 to 2047
- grid_first: float32 [78, 256], P(None, 'hid'), may hold values from -0.625 to 0.625
- wide_first: float32 [3, 512, 256], P(None, None, 'hid'), may hold values from -0.25 to 0.25
- second_layer: float32 [3, 256, 256], P(None, 'hid'), may hold values from -0.375 to 0.375
- decode_second: float32 [256, 78], P('hid'), may hold values from -0.375 to 0.375
- hidden_bias: float32 [4, 256], P(None, 'hid'), may hold values from -3 to 3
- norm_params: float32 [2, 3, 256], replicated, may hold values from 0.5 to 1.5
- decode_bias: float32 [78], replicated, may hold values from -2 to 2
- grid_first_avg: float32 [78, 256], P(None, 'hid'), may hold values from -0.0008544922 to 0.0008544922
- wide_first_avg: float32 [3, 512, 256], P(None, None, 'hid'), may hold values from -0.0008544922 to 0.0008544922
- second_layer_avg: float32 [3, 256, 256], P(None, 'hid'), may hold values from -0.0008544922 to 0.0008544922
- decode_second_avg: float32 [256, 78], P('hid'), may hold values from -0.0008544922 to 0.0008544922
- hidden_bias_avg: float32 [4, 256], P(None, 'hid'), may hold values from -0.0034179688 to 0.0034179688
- norm_params_avg: float32 [2, 3, 256], replicated, may hold values from -0.0034179688 to 0.0034179688
- decode_bias_avg: float32 [78], replicated, may hold values from -0.0034179688 to 0.0034179688
- grid_first_sq: float32 [78, 256], P(None, 'hid'), may hold values from 3.0517577e-09 to 1.2207031e-08
- wide_first_sq: float32 [3, 512, 256], P(None, None, 'hid'), may hold values from 3.0517577e-09 to 1.2207031e-08
- second_layer_sq: float32 [3, 256, 256], P(None, 'hid'), may hold values from 3.0517577e-09 to 1.2207031e-08
- decode_second_sq: float32 [256, 78], P('hid'), may hold values from 3.0517577e-09 to 1.2207031e-08
- hidden_bias_sq: float32 [4, 256], P(None, 'hid'), may hold values from 4.8828124e-08 to 1.953125e-07
- norm_params_sq: float32 [2, 3, 256], replicated, may hold values from 4.8828124e-08 to 1.953125e-07
- decode_bias_sq: float32 [78], replicated, may hold values from 4.8828124e-08 to 1.953125e-07
Outputs:
- loss_total: float32 [], replicated
- loss_weight: float32 [], replicated
- grid_first_new: float32 [78, 256], P(None, 'hid')
- wide_first_new: float32 [3, 512, 256], P(None, None, 'hid')
- second_layer_new: float32 [3, 256, 256], P(None, 'hid')
- decode_second_new: float32 [256, 78], P('hid')
- hidden_bias_new: float32 [4, 256], P(None, 'hid')
- norm_params_new: float32 [2, 3, 256], replicated
- decode_bias_new: float32 [78], replicated
- grid_first_avg_new: float32 [78, 256], P(None, 'hid')
- wide_first_avg_new: float32 [3, 512, 256], P(None, None, 'hid')
- second_layer_avg_new: float32 [3, 256, 256], P(None, 'hid')
- decode_second_avg_new: float32 [256, 78], P('hid')
- hidden_bias_avg_new: float32 [4, 256], P(None, 'hid')
- norm_params_avg_new: float32 [2, 3, 256], replicated
- decode_bias_avg_new: float32 [78], replicated
- grid_first_sq_new: float32 [78, 256], P(None, 'hid')
- wide_first_sq_new: float32 [3, 512, 256], P(None, None, 'hid')
- second_layer_sq_new: float32 [3, 256, 256], P(None, 'hid')
- decode_second_sq_new: float32 [256, 78], P('hid')
- hidden_bias_sq_new: float32 [4, 256], P(None, 'hid')
- norm_params_sq_new: float32 [2, 3, 256], replicated
- decode_bias_sq_new: float32 [78], replicated
- grid_first_half: bfloat16 [78, 256], P(None, 'hid')
- wide_first_half: bfloat16 [3, 512, 256], P(None, None, 'hid')
- second_layer_half: bfloat16 [3, 256, 256], P(None, 'hid')
- decode_second_half: bfloat16 [256, 78], P('hid')
Inputs may be any that keep to these rules, and one draw needn't show every extreme that they name: `live_points`: index 0 of rows holds 5461 live points, the last index 16384; the counts never fall along rows.
All inputs are finite; a program needn't handle non-finite values.
Results may differ from a plain program's by a relative error of at most 0.00145.
The roundings to bfloat16 on the way count: a program that leaves them out, or rounds other values in their place, can miss the bound.
Values may be sent and summed in bfloat16 or wider, within the bound.
A program may use at most 320 MiB of HBM per device.

v0:
```python
import jax
import jax.numpy as jnp
from jax import lax
from jax.sharding import PartitionSpec as P

STEP_COUNT = 5


def contract(left, right, left_dim, right_dim):
    return lax.dot_general(
        left, right, (((left_dim,), (right_dim,)), ((), ())), preferred_element_type=jnp.float32
    )


def mlp_forward(inputs, first, bias, second):
    pre = jnp.dot(inputs, first, preferred_element_type=jnp.float32) + bias
    act = jax.nn.silu(pre).astype(jnp.bfloat16)
    partial_out = jnp.dot(act, second, preferred_element_type=jnp.float32)
    summed = lax.psum_scatter(partial_out, "hid", scatter_dimension=0, tiled=True)
    return (pre, act, summed)


def norm_forward(values, gain, shift):
    centre = values - jnp.mean(values, -1, keepdims=True)
    scale = lax.rsqrt(jnp.mean(centre * centre, -1, keepdims=True) + 1e-05)
    normed = centre * scale
    return (normed * gain + shift, normed, scale)


def norm_backward(upstream, normed, scale, gain):
    gain_grad = jnp.sum(upstream * normed, 0)
    shift_grad = jnp.sum(upstream, 0)
    scaled = upstream * gain
    inner = (
        scaled
        - jnp.mean(scaled, -1, keepdims=True)
        - normed * jnp.mean(scaled * normed, -1, keepdims=True)
    )
    return (scale * inner, gain_grad, shift_grad)


def mlp_backward(upstream, inputs, pre, act, first, second, need_input):
    rounded = lax.all_gather(upstream.astype(jnp.bfloat16), "hid", axis=0, tiled=True)
    act_grad = contract(rounded, second, 1, 1)
    second_grad = contract(act, rounded, 0, 0)
    sigma = jax.nn.sigmoid(pre)
    pre_grad = (act_grad * sigma * (1.0 + pre * (1.0 - sigma))).astype(jnp.bfloat16)
    first_grad = contract(inputs, pre_grad, 0, 0)
    bias_grad = jnp.sum(pre_grad.astype(jnp.float32), 0)
    input_part = contract(pre_grad, first, 1, 1) if need_input else None
    return (input_part, first_grad, bias_grad, second_grad)


def input_share(input_part):
    return lax.psum_scatter(input_part, "hid", scatter_dimension=0, tiled=True)


def graph_sum(values, targets, count):
    whole = jax.ops.segment_sum(values, targets, num_segments=count)
    return lax.psum_scatter(whole, "hid", scatter_dimension=0, tiled=True)


def gather_rows(values):
    return lax.all_gather(values, "hid", axis=0, tiled=True)


def adamw(weight, avg, sq, grad, rate, decay):
    avg_new = 0.5 * avg + 0.5 * grad
    sq_new = 0.5 * sq + 0.5 * grad * grad
    fix = 1.0 - 0.5**STEP_COUNT
    step = avg_new / fix / (jnp.sqrt(sq_new / fix) + 1e-08)
    return (weight - rate * (step + decay * weight), avg_new, sq_new)


def body(
    grid_input,
    grid_target,
    live_points,
    level_weight,
    g2m_index,
    m2m_index,
    m2g_index,
    grid_first,
    wide_first,
    second_layer,
    decode_second,
    hidden_bias,
    norm_params,
    decode_bias,
    grid_first_avg,
    wide_first_avg,
    second_layer_avg,
    decode_second_avg,
    hidden_bias_avg,
    norm_params_avg,
    decode_bias_avg,
    grid_first_sq,
    wide_first_sq,
    second_layer_sq,
    decode_second_sq,
    hidden_bias_sq,
    norm_params_sq,
    decode_bias_sq,
):
    groups = lax.axis_size("hid")
    place = lax.axis_index("hid")

    def mine(values):
        count = values.shape[0] // groups
        return lax.dynamic_slice_in_dim(values, place * count, count, 0)

    grid_rows, channels = grid_input.shape
    mesh_rows, degree = m2m_index.shape
    latent = norm_params.shape[2]
    mesh_share = mesh_rows // groups
    grid_share = grid_rows // groups
    g2m_deg = g2m_index.shape[1]
    m2g_deg = m2g_index.shape[1]
    gfirst = grid_first.astype(jnp.bfloat16)
    wfirst = wide_first.astype(jnp.bfloat16)
    second = second_layer.astype(jnp.bfloat16)
    dsecond = decode_second.astype(jnp.bfloat16)
    gain = norm_params[0]
    shift = norm_params[1]
    pre_g, act_g, out_g = mlp_forward(grid_input, gfirst, hidden_bias[0], second[0])
    glat_mine, normed_g, scale_g = norm_forward(out_g, gain[0], shift[0])
    glat = gather_rows(glat_mine)
    h0 = jnp.mean(glat[g2m_index], 1)
    h0_mine = mine(h0)
    h0_half = h0.astype(jnp.bfloat16)
    recv = jnp.broadcast_to(h0_half[:, None, :], (mesh_rows, degree, latent))
    edge_in = jnp.concatenate([recv, h0_half[m2m_index]], -1).reshape(-1, 2 * latent)
    pre_e, act_e, out_e = mlp_forward(edge_in, wfirst[0], hidden_bias[1], second[1])
    elat, normed_e, scale_e = norm_forward(out_e, gain[1], shift[1])
    agg_mine = jnp.sum(elat.reshape(mesh_share, degree, latent), 1)
    node_in = jnp.concatenate([h0, gather_rows(agg_mine)], -1).astype(jnp.bfloat16)
    pre_n, act_n, out_n = mlp_forward(node_in, wfirst[1], hidden_bias[2], second[2])
    node_out, normed_n, scale_n = norm_forward(out_n, gain[2], shift[2])
    h1 = gather_rows(h0_mine + node_out)
    back = jnp.mean(h1[m2g_index], 1)
    dec_in = jnp.concatenate([glat, back], -1).astype(jnp.bfloat16)
    pre_d, act_d, out_d = mlp_forward(dec_in, wfirst[2], hidden_bias[3], dsecond)
    inputs_mine = mine(grid_input).astype(jnp.float32)
    target_mine = mine(grid_target).astype(jnp.float32)
    pred = inputs_mine + out_d + decode_bias
    row_ids = place * grid_share + lax.iota(jnp.int32, grid_share)
    mask = (row_ids < live_points[0]).astype(jnp.float32)[:, None]
    delta = (target_mine - inputs_mine) * mask
    square_sum, count = lax.psum((jnp.sum(delta * delta, 0), jnp.sum(mask)), ("rows", "hid"))
    var = square_sum / count + 1e-06
    weights = level_weight.astype(jnp.float32)
    loss_weight = count * jnp.sum(weights)
    err = pred - target_mine
    local_loss = jnp.sum(mask * weights * err * err / var)
    pred_grad = 2.0 * mask * weights * err / var / loss_weight
    back_d = mlp_backward(pred_grad, dec_in, pre_d, act_d, wfirst[2], dsecond, True)
    dec_grad = input_share(back_d[0])
    glat_grad = dec_grad[:, :latent]
    spread = jnp.broadcast_to(
        (dec_grad[:, latent:] / m2g_deg)[:, None, :], (grid_share, m2g_deg, latent)
    )
    h1_grad = graph_sum(spread.reshape(-1, latent), mine(m2g_index).reshape(-1), mesh_rows)
    node_grad, gain_n, shift_n = norm_backward(h1_grad, normed_n, scale_n, gain[2])
    back_n = mlp_backward(node_grad, node_in, pre_n, act_n, wfirst[1], second[2], True)
    node_in_grad = input_share(back_n[0])
    h0_grad = h1_grad + node_in_grad[:, :latent]
    elat_grad = jnp.broadcast_to(
        node_in_grad[:, None, latent:], (mesh_share, degree, latent)
    ).reshape(-1, latent)
    edge_grad, gain_e, shift_e = norm_backward(elat_grad, normed_e, scale_e, gain[1])
    back_e = mlp_backward(edge_grad, edge_in, pre_e, act_e, wfirst[0], second[1], True)
    edge_in_grad = input_share(back_e[0]).reshape(mesh_share, degree, 2 * latent)
    h0_grad = (
        h0_grad
        + jnp.sum(edge_in_grad[:, :, :latent], 1)
        + graph_sum(
            edge_in_grad[:, :, latent:].reshape(-1, latent), mine(m2m_index).reshape(-1), mesh_rows
        )
    )
    spread_h0 = jnp.broadcast_to((h0_grad / g2m_deg)[:, None, :], (mesh_share, g2m_deg, latent))
    glat_grad = glat_grad + graph_sum(
        spread_h0.reshape(-1, latent), mine(g2m_index).reshape(-1), grid_rows
    )
    grid_grad, gain_g, shift_g = norm_backward(glat_grad, normed_g, scale_g, gain[0])
    back_g = mlp_backward(grid_grad, grid_input, pre_g, act_g, gfirst, second[0], False)
    first_stack = jnp.stack([back_e[1], back_n[1], back_d[1]])
    second_stack = jnp.stack([back_g[3], back_e[3], back_n[3]])
    bias_stack = jnp.stack([back_g[2], back_e[2], back_n[2], back_d[2]])
    summed = lax.psum((back_g[1], first_stack, second_stack, back_d[3], bias_stack), "rows")
    norm_grad = jnp.stack(
        [jnp.stack([gain_g, gain_e, gain_n]), jnp.stack([shift_g, shift_e, shift_n])]
    )
    norm_sum, bias_sum, loss_total = lax.psum(
        (norm_grad, jnp.sum(pred_grad, 0), local_loss), ("rows", "hid")
    )
    grads = (summed[0], summed[1], summed[2], summed[3], summed[4], norm_sum, bias_sum)
    masters = (
        grid_first,
        wide_first,
        second_layer,
        decode_second,
        hidden_bias,
        norm_params,
        decode_bias,
    )
    avgs = (
        grid_first_avg,
        wide_first_avg,
        second_layer_avg,
        decode_second_avg,
        hidden_bias_avg,
        norm_params_avg,
        decode_bias_avg,
    )
    squares = (
        grid_first_sq,
        wide_first_sq,
        second_layer_sq,
        decode_second_sq,
        hidden_bias_sq,
        norm_params_sq,
        decode_bias_sq,
    )
    news, avg_news, sq_news = ([], [], [])
    for index in range(7):
        rate = 0.05 if index < 4 else 0.3
        decay = 0.1 if index < 4 else 0.0
        fresh, avg_new, sq_new = adamw(
            masters[index], avgs[index], squares[index], grads[index], rate, decay
        )
        news.append(fresh)
        avg_news.append(avg_new)
        sq_news.append(sq_new)
    return (
        loss_total,
        loss_weight,
        news[0],
        news[1],
        news[2],
        news[3],
        news[4],
        news[5],
        news[6],
        avg_news[0],
        avg_news[1],
        avg_news[2],
        avg_news[3],
        avg_news[4],
        avg_news[5],
        avg_news[6],
        sq_news[0],
        sq_news[1],
        sq_news[2],
        sq_news[3],
        sq_news[4],
        sq_news[5],
        sq_news[6],
        news[0].astype(jnp.bfloat16),
        news[1].astype(jnp.bfloat16),
        news[2].astype(jnp.bfloat16),
        news[3].astype(jnp.bfloat16),
    )


def solution(mesh):
    in_specs = (
        P("rows", None),
        P("rows", None),
        P("rows"),
        P(),
        P("rows", None),
        P("rows", None),
        P("rows", None),
        P(None, "hid"),
        P(None, None, "hid"),
        P(None, "hid", None),
        P("hid", None),
        P(None, "hid"),
        P(),
        P(),
        P(None, "hid"),
        P(None, None, "hid"),
        P(None, "hid", None),
        P("hid", None),
        P(None, "hid"),
        P(),
        P(),
        P(None, "hid"),
        P(None, None, "hid"),
        P(None, "hid", None),
        P("hid", None),
        P(None, "hid"),
        P(),
        P(),
    )
    out_specs = (
        P(),
        P(),
        P(None, "hid"),
        P(None, None, "hid"),
        P(None, "hid", None),
        P("hid", None),
        P(None, "hid"),
        P(),
        P(),
        P(None, "hid"),
        P(None, None, "hid"),
        P(None, "hid", None),
        P("hid", None),
        P(None, "hid"),
        P(),
        P(),
        P(None, "hid"),
        P(None, None, "hid"),
        P(None, "hid", None),
        P("hid", None),
        P(None, "hid"),
        P(),
        P(),
        P(None, "hid"),
        P(None, None, "hid"),
        P(None, "hid", None),
        P("hid", None),
    )
    return jax.shard_map(body, mesh=mesh, in_specs=in_specs, out_specs=out_specs, check_vma=False)
```

profile of v0, /device:TPU:0, one launch (start us, length us, event | category | flops | bytes accessed | tf_op | source)
XLA Modules:
  0.0 2228.7 jit_solution(17232055324340271890)
XLA Ops:
  14.0 8.1 fusion.36
  22.9 128.2 %reduce-scatter.11.cloned.1.call-done = f32[4096,256]{1,0:T(8,128)} async-done(((f32[16384,256]{1,0:T(8,128)}), f32[4096,256]{1,0:T(8,128)}) %reduce-scatter.11.cloned.1.call-update) | async-done | bytes 4194320 | tf_op jit(solution)/shard_map/reduce_scatter | solution.py:19
  164.5 103.1 %all-gather.8.cloned.1.call-done = f32[16384,256]{1,0:T(8,128)} async-done(((f32[4096,256]{1,0:T(8,128)}), f32[16384,256]{1,0:T(8,128)}) %all-gather.8.cloned.1.call-update) | async-done | bytes 16777232 | tf_op jit(solution)/shard_map/all_gather | solution.py:64
  267.6 67.8 %gather_fusion = f32[16384,256]{1,0:T(8,128)} fusion(f32[16384,256]{1,0:T(8,128)} %all-gather.8.cloned.1.call-done, s32[16384]{0:T(1024)S(1)} %broadcast_clamp_fusion.1), kind=kCustom, calls=%fused_computation | custom fusion | bytes 33619968 | tf_op jit(solution)/shard_map/gather | solution.py:128
  335.4 11.0 bitcast_reduce_fusion
  346.6 49.2 %gather_fusion.1 = bf16[12288,256]{1,0:T(8,128)(2,1)} fusion(bf16[2048,256]{1,0:T(8,128)(2,1)S(1)} %get-tuple-element.109, s32[12288]{0:T(1024)S(1)} %broadcast_clamp_fusion.2), kind=kCustom, calls=%fused_computation.1 | custom fusion | bytes 12632064 | tf_op jit(solution)/shard_map/gather | solution.py:132
  395.8 11.3 reshape.194
  410.5 7.6 pad_maximum_fusion
  418.0 21.2 reshape.178
  439.3 8.4 convolution_add_fusion.2
  449.3 6.4 fusion.37
  456.2 98.8 %reduce-scatter.13.cloned.1.call-done = f32[3072,256]{1,0:T(8,128)} async-done(((f32[12288,256]{1,0:T(8,128)}), f32[3072,256]{1,0:T(8,128)}) %reduce-scatter.13.cloned.1.call-update) | async-done | bytes 3145744 | tf_op jit(solution)/shard_map/reduce_scatter | solution.py:19
  572.0 16.8 all-gather.10.cloned.1.call-done
  593.6 31.5 %reduce-scatter.15.cloned.1.call-done = f32[512,256]{1,0:T(8,128)} async-done(((f32[2048,256]{1,0:T(8,128)}), f32[512,256]{1,0:T(8,128)}) %reduce-scatter.15.cloned.1.call-update) | async-done | bytes 524304 | tf_op jit(solution)/shard_map/reduce_scatter | solution.py:19
  635.0 7.5 reshape.203
  642.5 8.9 convert.12
  652.5 185.8 %gather_fusion.2 = f32[49152,256]{1,0:T(8,128)} fusion(f32[2048,256]{1,0:T(8,128)} %all-gather.12.cloned.1.call-done, s32[49152]{0:T(1024)S(1)} %broadcast_clamp_fusion), kind=kCustom, calls=%fused_computation.2 | custom fusion | bytes 100859904 | tf_op jit(solution)/shard_map/gather | solution.py:140
  838.3 72.9 %reshape.206 = f32[16384,3,256]{2,1,0:T(4,128)} reshape(f32[49152,256]{1,0:T(8,128)} %gather_fusion.2) | data formatting | bytes 100663296 | tf_op jit(solution)/shard_map/gather | solution.py:140
  911.2 94.3 %reduce_sum.287 = f32[16384,256]{1,0:T(8,128)} reduce(f32[16384,3,256]{2,1,0:T(4,128)} %reshape.206, f32[]{:T(128)} %constant.41.clone.1), dimensions={1}, to_apply=%region_11.12 | reduce | flops 8388608 | bytes 67108864 | tf_op jit(solution)/shard_map/reduce_sum | solution.py:140
  1005.5 10.3 multiply_convert_fusion
  1016.8 8.9 multiply_convert_fusion.2
  1033.5 39.9 %all-reduce.1 = (f32[78]{0:T(128)S(1)}, f32[]{:T(128)}) all-reduce(f32[78]{0:T(128)S(1)} %fusion.17, f32[]{:T(128)} %fusion.48), channel_id=1, replica_groups=mesh['rows'=8,'hid'=4] {'rows','hid'}, use_global_device_ids=true, to_apply=%region_14.15 | all-reduce | flops 79 | bytes 632 | tf_op jit(solution)/shard_map/psum | solution.py:149
  1075.9 6.6 reduce-scatter.17.cloned.1.call-done
  1086.5 25.5 %all-gather.14.cloned.1.call-done = bf16[16384,78]{0,1:T(8,128)(2,1)} async-done(((bf16[4096,78]{0,1:T(8,128)(2,1)}), bf16[16384,78]{0,1:T(8,128)(2,1)}) %all-gather.14.cloned.1.call-update) | async-done | bytes 2555920 | tf_op jit(solution)/shard_map/all_gather | solution.py:43
  1119.1 13.1 fusion.33
  1135.1 232.1 %reduce-scatter.19.cloned.1.call-done = f32[4096,512]{1,0:T(8,128)} async-done(((f32[16384,512]{1,0:T(8,128)}), f32[4096,512]{1,0:T(8,128)}) %reduce-scatter.19.cloned.1.call-update) | async-done | bytes 8388624 | tf_op jit(solution)/shard_map/reduce_scatter | solution.py:55
  1369.7 7.5 broadcast_in_dim.21
  1377.2 19.7 reshape.213
  1397.0 67.9 %scatter_custom_fusion = f32[2048,256]{1,0:T(8,128)} fusion(s32[12288]{0:T(1024)S(1)} %reshape.211, f32[12288,256]{1,0:T(8,128)} %reshape.213, f32[]{:T(128)} %constant.41.clone.1), kind=kCustom, calls=%fused_computation.80 | custom fusion | flops 3145728 | bytes 2097664 | tf_op jit(solution)/shard_map/scatter-add | solution.py:59
  1465.0 31.5 %reduce-scatter.21.cloned.1.call-done = f32[512,256]{1,0:T(8,128)} async-done(((f32[2048,256]{1,0:T(8,128)}), f32[512,256]{1,0:T(8,128)}) %reduce-scatter.21.cloned.1.call-update) | async-done | bytes 524304 | tf_op jit(solution)/shard_map/reduce_scatter | solution.py:60
  1500.1 16.8 all-gather.16.cloned.1.call-done
  1521.7 44.4 %reduce-scatter.23.cloned.1.call-done = f32[512,512]{1,0:T(8,128)} async-done(((f32[2048,512]{1,0:T(8,128)}), f32[512,512]{1,0:T(8,128)}) %reduce-scatter.23.cloned.1.call-update) | async-done | bytes 1048592 | tf_op jit(solution)/shard_map/reduce_scatter | solution.py:55
  1582.4 46.5 %all-gather.18.cloned.1.call-done = bf16[12288,256]{1,0:T(8,128)(2,1)} async-done(((bf16[3072,256]{1,0:T(8,128)(2,1)}), bf16[12288,256]{1,0:T(8,128)(2,1)}) %all-gather.18.cloned.1.call-update) | async-done | bytes 6291472 | tf_op jit(solution)/shard_map/all_gather | solution.py:43
  1628.9 5.8 convert_reduce_fusion.2
  1636.0 10.1 fusion.31
  1647.2 179.5 %reduce-scatter.25.cloned.1.call-done = f32[3072,512]{1,0:T(8,128)} async-done(((f32[12288,512]{1,0:T(8,128)}), f32[3072,512]{1,0:T(8,128)}) %reduce-scatter.25.cloned.1.call-update) | async-done | bytes 6291472 | tf_op jit(solution)/shard_map/reduce_scatter | solution.py:55
  1826.7 8.3 reshape.182
  1845.3 18.9 scatter_custom_fusion.1
  1865.7 30.1 %reduce-scatter.27.cloned.1.call-done = f32[512,256]{1,0:T(8,128)} async-done(((f32[2048,256]{1,0:T(8,128)}), f32[512,256]{1,0:T(8,128)}) %reduce-scatter.27.cloned.1.call-update) | async-done | bytes 524304 | tf_op jit(solution)/shard_map/reduce_scatter | solution.py:60
  1897.1 29.4 %scatter_custom_fusion.2 = f32[16384,256]{1,0:T(8,128)} fusion(s32[4096]{0:T(1024)S(1)} %reshape.227, f32[]{:T(128)} %constant.41.clone.1, f32[512,256]{1,0:T(8,128)S(1)} %fusion.28), kind=kCustom, calls=%fused_computation.23 | custom fusion | flops 1048576 | bytes 17301508 | tf_op jit(solution)/shard_map/scatter-add | solution.py:59
  1926.5 126.2 %reduce-scatter.29.cloned.1.call-done = f32[4096,256]{1,0:T(8,128)} async-done(((f32[16384,256]{1,0:T(8,128)}), f32[4096,256]{1,0:T(8,128)}) %reduce-scatter.29.cloned.1.call-update) | async-done | bytes 4194320 | tf_op jit(solution)/shard_map/reduce_scatter | solution.py:60
  2052.8 6.2 multiply_reduce_fusion
  2066.2 9.8 fusion.21
  2077.5 7.2 convolution_bitcast_fusion
  2086.7 40.1 %all-reduce = (f32[]{:T(128)}, f32[2,3,256]{2,1,0:T(4,128)S(1)}, f32[78]{0:T(128)S(1)}) all-reduce(f32[]{:T(128)} %get-tuple-element.108, f32[2,3,256]{2,1,0:T(4,128)S(1)} %pad_maximum_fusion.13, f32[78]{0:T(128)S(1)} %get-tuple-element.101), channel_id=1, replica_groups=mesh['rows'=8,'hid'=4] {'rows','hid'}, use_global_device_ids=true, to_apply=%region_18.19 | all-reduce | flops 1615 | bytes 12920 | tf_op jit(solution)/shard_map/psum | solution.py:193
  2129.2 7.5 convert_reduce_fusion.1
  2141.5 38.5 %all-reduce.2 = (f32[78,64]{0,1:T(8,128)S(1)}, f32[64,78]{1,0:T(8,128)S(1)}, f32[4,64]{1,0:T(4,128)S(1)}) all-reduce(f32[78,64]{0,1:T(8,128)S(1)} %convolution_bitcast_fusion.4, f32[64,78]{1,0:T(8,128)S(1)} %fusion.69, f32[4,64]{1,0:T(4,128)S(1)} %pad_maximum_fusion.14), channel_id=1, replica_groups=mesh['rows'=8,'hid'=4] {'rows'}, use_global_device_ids=true, to_apply=%region_36.37 | all-reduce | flops 10240 | bytes 81920 | tf_op jit(solution)/shard_map/psum | solution.py:189
  2182.0 34.4 %all-reduce.6.cloned.1.call-done = (f32[3,512,64]{1,2,0:T(8,128)}, f32[3,64,256]{2,1,0:T(8,128)}) async-done(((f32[3,512,64]{1,2,0:T(8,128)}, f32[3,64,256]{2,1,0:T(8,128)}), (f32[3,512,64]{1,2,0:T(8,128)}, f32[3,64,256]{2,1,0:T(8,128)})) %all-reduce.6.cloned.1.call-update) | async-done | bytes 589840 | tf_op jit(solution)/shard_map/psum | solution.py:189
  (310 shorter events, 148.2 us)
Async XLA Ops:
  7.2 143.9 %reduce-scatter.11.cloned.1.call-start = ((), (), s32[]{:S(2)}) async-start(), calls=%async_computation.10 | async-start | bytes 20971520 | tf_op jit(solution)/shard_map/reduce_scatter | solution.py:19
  9.5 581.3 %copy-start.35 = (bf16[3,64,256]{2,1,0:T(8,128)(2,1)}, bf16[3,64,256]{2,1,0:T(8,128)(2,1)S(1)}, u32[]{:S(2)}) copy-start(bf16[3,64,256]{2,1,0:T(8,128)(2,1)S(1)} %convert_element_type.102) | copy-start | bytes 294916
  22.2 245.4 %all-gather.8.cloned.1.call-start = ((), (), s32[]{:S(2)}) async-start(), calls=%async_computation.11 | async-start | bytes 20971520 | tf_op jit(solution)/shard_map/all_gather | solution.py:64
  22.9 134.3 %copy-start.68 = (f32[1,1,256]{2,0,1:T(1,128)}, f32[1,1,256]{2,0,1:T(1,128)S(1)}, u32[]{:S(2)}) copy-start(f32[1,1,256]{2,0,1:T(1,128)S(1)} %get-tuple-element.115) | copy-start | bytes 3076
  22.9 537.5 %copy-start.62 = (f32[1,1,256]{2,0,1:T(1,128)}, f32[1,1,256]{2,0,1:T(1,128)S(1)}, u32[]{:S(2)}) copy-start(f32[1,1,256]{2,0,1:T(1,128)S(1)} %get-tuple-element.113) | copy-start | bytes 3076
  22.9 604.7 %copy-start.66 = (f32[1,1,256]{2,0,1:T(1,128)}, f32[1,1,256]{2,0,1:T(1,128)S(1)}, u32[]{:S(2)}) copy-start(f32[1,1,256]{2,0,1:T(1,128)S(1)} %get-tuple-element.111) | copy-start | bytes 3076
  161.5 393.5 %reduce-scatter.13.cloned.1.call-start = ((), (), s32[]{:S(2)}) async-start(), calls=%async_computation.12 | async-start | bytes 15728640 | tf_op jit(solution)/shard_map/reduce_scatter | solution.py:19
  162.5 426.3 %copy-start.25 = (bf16[3,512,64]{1,2,0:T(8,128)(2,1)}, bf16[3,512,64]{1,2,0:T(8,128)(2,1)S(1)}, u32[]{:S(2)}) copy-start(bf16[3,512,64]{1,2,0:T(8,128)(2,1)S(1)} %convert_element_type.103) | copy-start | bytes 589828
  346.6 242.3 %copy-start = (bf16[2048,256]{1,0:T(8,128)(2,1)}, bf16[2048,256]{1,0:T(8,128)(2,1)S(1)}, u32[]{:S(2)}) copy-start(bf16[2048,256]{1,0:T(8,128)(2,1)S(1)} %get-tuple-element.109) | copy-start | bytes 3145732
  455.7 133.1 %all-gather.10.cloned.1.call-start = ((), (), s32[]{:S(2)}) async-start(), calls=%async_computation.13 | async-start | bytes 1310720 | tf_op jit(solution)/shard_map/all_gather | solution.py:64
  572.0 53.1 %reduce-scatter.15.cloned.1.call-start = ((), (), s32[]{:S(2)}) async-start(), calls=%async_computation.14 | async-start | bytes 2621440 | tf_op jit(solution)/shard_map/reduce_scatter | solution.py:19
  593.5 59.0 %all-gather.12.cloned.1.call-start = ((), (), s32[]{:S(2)}) async-start(), calls=%async_computation.15 | async-start | bytes 2621440 | tf_op jit(solution)/shard_map/all_gather | solution.py:64
  629.7 452.8 %reduce-scatter.17.cloned.1.call-start = ((), (), s32[]{:S(2)}) async-start(), calls=%async_computation.16 | async-start | bytes 6553600 | tf_op jit(solution)/shard_map/reduce_scatter | solution.py:19
  1030.3 52.3 %copy-start.73 = (f32[78]{0:T(128)S(1)}, f32[78]{0:T(128)}, u32[]{:S(2)}) copy-start(f32[78]{0:T(128)} %param.41) | copy-start | bytes 940
  1030.3 81.7 %all-gather.14.cloned.1.call-start = ((), (), s32[]{:S(2)}) async-start(), calls=%async_computation.17 | async-start | bytes 3276800 | tf_op jit(solution)/shard_map/all_gather | solution.py:43
  1086.3 280.9 %reduce-scatter.19.cloned.1.call-start = ((), (), s32[]{:S(2)}) async-start(), calls=%async_computation.18 | async-start | bytes 41943040 | tf_op jit(solution)/shard_map/reduce_scatter | solution.py:55
  1132.2 364.3 %reduce-scatter.21.cloned.1.call-start = ((), (), s32[]{:S(2)}) async-start(), calls=%async_computation.19 | async-start | bytes 2621440 | tf_op jit(solution)/shard_map/reduce_scatter | solution.py:60
  1397.0 99.5 %copy-start.14 = (f32[512,256]{1,0:T(8,128)S(1)}, f32[512,256]{1,0:T(8,128)}, u32[]{:S(2)}) copy-start(f32[512,256]{1,0:T(8,128)} %reduce-scatter.15.cloned.1.call-done) | copy-start | bytes 1572868
  1397.0 99.5 %copy-start.55 = (f32[512]{0:T(512)S(1)}, f32[512]{0:T(512)}, u32[]{:S(2)}) copy-start(f32[512]{0:T(512)} %copy-done.54) | copy-start | bytes 6148
  1397.0 99.5 %copy-start.57 = (f32[512]{0:T(512)S(1)}, f32[512]{0:T(512)}, u32[]{:S(2)}) copy-start(f32[512]{0:T(512)} %copy-done.56) | copy-start | bytes 6148
  1397.0 99.5 %copy-start.67 = (f32[1,1,256]{2,0,1:T(1,128)S(1)}, f32[1,1,256]{2,0,1:T(1,128)}, u32[]{:S(2)}) copy-start(f32[1,1,256]{2,0,1:T(1,128)} %copy-done.66) | copy-start | bytes 3076
  1397.0 120.0 %copy-start.30 = (f32[2048,64]{0,1:T(8,128)S(1)}, f32[2048,64]{0,1:T(8,128)}, u32[]{:S(2)}) copy-start(f32[2048,64]{0,1:T(8,128)} %copy-done.29) | copy-start | bytes 1572868
  1397.0 119.9 %copy-start.36 = (bf16[3,64,256]{2,1,0:T(8,128)(2,1)S(1)}, bf16[3,64,256]{2,1,0:T(8,128)(2,1)}, u32[]{:S(2)}) copy-start(bf16[3,64,256]{2,1,0:T(8,128)(2,1)} %copy-done.35) | copy-start | bytes 294916
  1464.9 52.0 %all-gather.16.cloned.1.call-start = ((), (), s32[]{:S(2)}) async-start(), calls=%async_computation.20 | async-start | bytes 1310720 | tf_op jit(solution)/shard_map/all_gather | solution.py:43
  1500.1 66.1 %reduce-scatter.23.cloned.1.call-start = ((), (), s32[]{:S(2)}) async-start(), calls=%async_computation.21 | async-start | bytes 5242880 | tf_op jit(solution)/shard_map/reduce_scatter | solution.py:55
  1518.7 48.5 %copy-start.63 = (f32[1,1,256]{2,0,1:T(1,128)S(1)}, f32[1,1,256]{2,0,1:T(1,128)}, u32[]{:S(2)}) copy-start(f32[1,1,256]{2,0,1:T(1,128)} %copy-done.62) | copy-start | bytes 3076
  1521.5 107.5 %all-gather.18.cloned.1.call-start = ((), (), s32[]{:S(2)}) async-start(), calls=%async_computation.22 | async-start | bytes 7864320 | tf_op jit(solution)/shard_map/all_gather | solution.py:43
  1582.4 244.3 %reduce-scatter.25.cloned.1.call-start = ((), (), s32[]{:S(2)}) async-start(), calls=%async_computation.23 | async-start | bytes 31457280 | tf_op jit(solution)/shard_map/reduce_scatter | solution.py:55
  1646.1 249.8 %reduce-scatter.27.cloned.1.call-start = ((), (), s32[]{:S(2)}) async-start(), calls=%async_computation.24 | async-start | bytes 2621440 | tf_op jit(solution)/shard_map/reduce_scatter | solution.py:60
  1845.3 50.5 %copy-start.20 = (f32[512,256]{1,0:T(8,128)S(1)}, f32[512,256]{1,0:T(8,128)}, u32[]{:S(2)}) copy-start(f32[512,256]{1,0:T(8,128)} %reduce-scatter.21.cloned.1.call-done) | copy-start | bytes 1572868
  1845.3 50.5 %copy-start.27 = (f32[512,512]{1,0:T(8,128)S(1)}, f32[512,512]{1,0:T(8,128)}, u32[]{:S(2)}) copy-start(f32[512,512]{1,0:T(8,128)} %reduce-scatter.23.cloned.1.call-done) | copy-start | bytes 3145732
  1864.3 188.5 %reduce-scatter.29.cloned.1.call-start = ((), (), s32[]{:S(2)}) async-start(), calls=%async_computation.25 | async-start | bytes 20971520 | tf_op jit(solution)/shard_map/reduce_scatter | solution.py:60
  1926.5 126.3 %copy-start.33 = (f32[4096]{0:T(1024)S(1)}, f32[4096]{0:T(1024)}, u32[]{:S(2)}) copy-start(f32[4096]{0:T(1024)} %copy-done.32) | copy-start | bytes 49156
  1926.5 126.3 %copy-start.42 = (f32[4096]{0:T(1024)S(1)}, f32[4096]{0:T(1024)}, u32[]{:S(2)}) copy-start(f32[4096]{0:T(1024)} %copy-done.41) | copy-start | bytes 49156
  1926.5 126.3 %copy-start.69 = (f32[1,1,256]{2,0,1:T(1,128)S(1)}, f32[1,1,256]{2,0,1:T(1,128)}, u32[]{:S(2)}) copy-start(f32[1,1,256]{2,0,1:T(1,128)} %copy-done.68) | copy-start | bytes 3076
  1926.5 202.7 %all-gather.20.cloned.1.call-start = ((), (), s32[]{:S(2)}) async-start(), calls=%async_computation.26 | async-start | bytes 10485760 | tf_op jit(solution)/shard_map/all_gather | solution.py:43
  2063.3 153.1 %all-reduce.6.cloned.1.call-start = ((), (), s32[]{:S(2)}) async-start(), calls=%async_computation.27 | async-start | bytes 1179648 | tf_op jit(solution)/shard_map/psum | solution.py:189
  2085.5 43.2 %copy-start.76 = (f32[78]{0:T(128)S(1)}, f32[78]{0:T(128)}, u32[]{:S(2)}) copy-start(f32[78]{0:T(128)} %param.48) | copy-start | bytes 940
  2085.5 43.2 %copy-start.77 = (f32[78]{0:T(128)S(1)}, f32[78]{0:T(128)}, u32[]{:S(2)}) copy-start(f32[78]{0:T(128)} %param.55) | copy-start | bytes 940
  2139.0 42.3 %copy-start.51 = (f32[64,78]{1,0:T(8,128)S(1)}, f32[64,78]{1,0:T(8,128)}, u32[]{:S(2)}) copy-start(f32[64,78]{1,0:T(8,128)} %param.38) | copy-start | bytes 59908
  2139.1 42.3 %copy-start.60 = (f32[64,78]{1,0:T(8,128)S(1)}, f32[64,78]{1,0:T(8,128)}, u32[]{:S(2)}) copy-start(f32[64,78]{1,0:T(8,128)} %param.45) | copy-start | bytes 59908
  2139.1 42.3 %copy-start.61 = (f32[64,78]{1,0:T(8,128)S(1)}, f32[64,78]{1,0:T(8,128)}, u32[]{:S(2)}) copy-start(f32[64,78]{1,0:T(8,128)} %param.52) | copy-start | bytes 59908
  2139.1 77.3 %copy-start.28 = (f32[3,64,256]{2,1,0:T(8,128)S(1)}, f32[3,64,256]{2,1,0:T(8,128)}, u32[]{:S(2)}) copy-start(f32[3,64,256]{2,1,0:T(8,128)} %param.37) | copy-start | bytes 589828
  2139.1 77.3 %copy-start.45 = (f32[3,64,256]{2,1,0:T(8,128)S(1)}, f32[3,64,256]{2,1,0:T(8,128)}, u32[]{:S(2)}) copy-start(f32[3,64,256]{2,1,0:T(8,128)} %param.44) | copy-start | bytes 589828
  2139.1 77.3 %copy-start.46 = (f32[3,64,256]{2,1,0:T(8,128)S(1)}, f32[3,64,256]{2,1,0:T(8,128)}, u32[]{:S(2)}) copy-start(f32[3,64,256]{2,1,0:T(8,128)} %param.51) | copy-start | bytes 589828
  2139.1 79.1 %copy-start.24 = (f32[3,512,64]{1,2,0:T(8,128)S(1)}, f32[3,512,64]{1,2,0:T(8,128)}, u32[]{:S(2)}) copy-start(f32[3,512,64]{1,2,0:T(8,128)} %param.36) | copy-start | bytes 1179652
  2139.1 79.1 %copy-start.37 = (f32[3,512,64]{1,2,0:T(8,128)S(1)}, f32[3,512,64]{1,2,0:T(8,128)}, u32[]{:S(2)}) copy-start(f32[3,512,64]{1,2,0:T(8,128)} %param.43) | copy-start | bytes 1179652
  2139.1 79.1 %copy-start.38 = (f32[3,512,64]{1,2,0:T(8,128)S(1)}, f32[3,512,64]{1,2,0:T(8,128)}, u32[]{:S(2)}) copy-start(f32[3,512,64]{1,2,0:T(8,128)} %param.50) | copy-start | bytes 1179652
  (56 other events, 645.4 us)
Sparse Core Ops, SparseCore 0:
  22.3 128.7 reduce-scatter.10
  161.6 105.9 all-gather.7
  455.9 99.0 reduce-scatter.12
  572.1 16.7 all-gather.9
  593.6 31.4 reduce-scatter.14
  629.8 22.5 all-gather.11
  1030.4 52.0 reduce-scatter.16
  1086.4 25.5 all-gather.13
  1132.4 234.7 reduce-scatter.18
  1465.0 31.4 reduce-scatter.20
  1500.2 16.7 all-gather.15
  1521.6 44.4 reduce-scatter.22
  1582.5 46.3 all-gather.17
  1646.2 180.4 reduce-scatter.24
  1864.4 31.4 reduce-scatter.26
  1926.6 126.0 reduce-scatter.28
  2063.5 59.0 all-gather.19
  2141.6 74.7 all-reduce.5
where the time goes:
time: 2240 us; the launch traced here: 2230 us
  waiting for transfers between devices  1150 us (51%)
  local copies, waits for them, and re-layouts  501 us (22%)
  other arithmetic  323 us (14%)
  blocking collectives  118 us (5%)
  matrix products  112 us (5%)
    reduce_scatter x3, waiting for transfers between devices, input_share(): return lax.psum_scatter(input_part, 'hid', scatter_dimension=0, tiled=True)  456 us
    reduce_scatter x4, waiting for transfers between devices, mlp_forward(): lax.psum_scatter(partial_out, 'hid', scatter_dimension=0, tiled=True)  265 us
    gather x2, local copies, waits for them, and re-layouts, body(): back = jnp.mean(h1[m2g_index], 1)  259 us
    reduce_scatter x3, waiting for transfers between devices, graph_sum(): return lax.psum_scatter(whole, 'hid', scatter_dimension=0, tiled=True)  188 us
    all_gather x3, waiting for transfers between devices, gather_rows(): return lax.all_gather(values, 'hid', axis=0, tiled=True)  121 us
    scatter-add x3, other arithmetic, graph_sum(): whole = jax.ops.segment_sum(values, targets, num_segments=count)  116 us
    reduce_sum x1, other arithmetic, body(): back = jnp.mean(h1[m2g_index], 1)  94.3 us
    all_gather x4, waiting for transfers between devices, mlp_backward(): lax.all_gather(upstream.astype(jnp.bfloat16), 'hid', axis=0, tiled=True)  88.8 us
  transfers between devices with their start and end apart: 18, of which 17 were waited for; matrix products, arithmetic and copies ran while one was open for 3% of the time, Pallas kernels for 0%

commit v1 on v0

v1 whole, which is shorter than its diff:
```python
import functools

import jax
import jax.numpy as jnp
from jax import lax
from jax.experimental import pallas as pl
from jax.experimental.pallas import tpu as pltpu
from jax.sharding import PartitionSpec as P

STEP_COUNT = 5
MESH = pl.DeviceIdType.MESH
bf16 = jnp.bfloat16
f32 = jnp.float32
TILE = 512
PAD = 80
COLS = {"g1": 0, "g2": 128, "e1": 384, "e2": 896, "n1": 1152, "n2": 1664, "d1": 1920, "d2": 2432}
GROUPS = {"g": (0, 384), "e": (384, 768), "n": (1152, 768), "d": (1920, 640)}
PACK = 2560


def mm(left, right):
    return lax.dot_general(left, right, (((1,), (0,)), ((), ())), preferred_element_type=f32)


def mt(left, right):
    return lax.dot_general(left, right, (((1,), (1,)), ((), ())), preferred_element_type=f32)


def flip(values):
    return values.astype(f32).T.astype(bf16)


def split2(values):
    high = values.astype(bf16)
    low = (values - high.astype(f32)).astype(bf16)
    return high, low


def fold(values):
    total = values[:, :128]
    for at in range(128, values.shape[1], 128):
        total = total + values[:, at : at + 128]
    return total


def ones_at(index, base, rows):
    lanes = index.shape[1]
    local = lax.broadcasted_iota(jnp.int32, (256, lanes), 0).astype(f32).astype(bf16)
    parts = []
    for block in range(rows // 256):
        total = None
        for k in range(index.shape[0]):
            shifted = (index[k : k + 1] - (base + block * 256)).astype(f32).astype(bf16)
            hit = jnp.where(
                jnp.broadcast_to(shifted, (256, lanes)) == local,
                jnp.asarray(1, bf16),
                jnp.asarray(0, bf16),
            )
            total = hit if total is None else total + hit
        parts.append(total)
    return parts


def act_forward(pre):
    sigma = 0.5 * jnp.tanh(0.5 * pre) + 0.5
    act = pre * sigma
    return act.astype(bf16), sigma + act * (1.0 - sigma)


def norm_forward(values):
    size = values.shape[0]
    centre = values - jnp.sum(values, 0, keepdims=True) * (1.0 / size)
    var = jnp.sum(centre * centre, 0, keepdims=True) * (1.0 / size)
    scale = lax.rsqrt(var + 1e-05)
    return centre * scale, scale


def norm_backward(upstream, normed, scale, gain):
    size = upstream.shape[0]
    scaled = upstream * gain
    first = jnp.sum(scaled, 0, keepdims=True) * (1.0 / size)
    second = jnp.sum(scaled * normed, 0, keepdims=True) * (1.0 / size)
    return scale * (scaled - first - normed * second)


def pick_kernel(place_ref, index_ref, xt_ref, tt_ref, xm_ref, tm_ref, xg_ref, rows, got):
    grid_rows = xt_ref.shape[1]
    channels = xt_ref.shape[0]
    degree, share = index_ref.shape
    mine = xm_ref.shape[1]

    def padded(values, to):
        return jnp.concatenate(
            [values.astype(f32), jnp.zeros((to - channels, values.shape[1]), f32)], 0
        )

    def turn(i, carry):
        at = pl.multiple_of(i * TILE, TILE)
        rows[pl.ds(at, TILE), :] = padded(xt_ref[:, pl.ds(at, TILE)], 128).T
        return carry

    lax.fori_loop(0, grid_rows // TILE, turn, 0)
    step = 16
    for k in range(degree):

        def pick(i, carry):
            for u in range(step):
                got[pl.ds(k * share + i * step + u, 1), :] = rows[
                    pl.ds(index_ref[k, i * step + u], 1), :
                ]
            return carry

        lax.fori_loop(0, share // step, pick, 0)

    def back(i, carry):
        at = pl.multiple_of(i * TILE, TILE)
        here = pl.ds(at, TILE)
        there = pl.ds(pl.multiple_of(place_ref[0] * mine + i * TILE, TILE), TILE)
        xg_ref[:, here] = got[here, :].T[:PAD].astype(bf16)
        xm_ref[:, here] = padded(xt_ref[:, there], PAD).astype(bf16)
        tm_ref[:, here] = padded(tt_ref[:, there], PAD).astype(bf16)
        return carry

    lax.fori_loop(0, mine // TILE, back, 0)


class Mail:
    def __init__(self, send, recv):
        self.send, self.recv, self.used = send, recv, 0

    def copy(self, source, target, device):
        at = self.used
        self.used += 1
        if self.send is None:
            return None
        copy = pltpu.make_async_remote_copy(
            src_ref=source,
            dst_ref=target,
            send_sem=self.send.at[at],
            recv_sem=self.recv.at[at],
            device_id=device,
            device_id_type=MESH,
        )
        copy.start()
        return copy


def count_copies(row_groups):
    near = min(row_groups, 8)
    far = row_groups // near
    sums = 3 + (row_groups - 1)
    rows_sum = 2 * (near - 1) + (far - 1)
    return 15 + 9 + 8 + sums + 4 * (4 + rows_sum) + 3


def main_kernel(
    live_ref,
    x_ref,
    t_ref,
    xg_ref,
    g2m_ref,
    m2m_ref,
    m2g_ref,
    wown_ref,
    bown_ref,
    norm_ref,
    chan_ref,
    out_ref,
    all_ref,
    tot_ref,
    w,
    wt,
    bias,
    h0full,
    h1full,
    hgfull,
    onehot,
    ds_g,
    act_g,
    nrm_g,
    scale_g,
    dec_in,
    dp_d,
    dglat,
    ds_e,
    act_e,
    hs_e,
    nrm_e,
    scale_e,
    dsum,
    land_a,
    land_b,
    grad,
    gland_a,
    gland_b,
    held,
    rland,
    fland,
    nacc,
    bacc,
    cacc,
    h0_mine,
    node_in,
    mesh_tmp,
    small,
    sland_h,
    sland_r,
    send,
    recv,
    *,
    row_groups,
    g2m_deg,
    m2g_deg,
):
    hid = lax.axis_index("hid")
    row = lax.axis_index("rows")
    near = min(row_groups, 8)
    far = row_groups // near
    row_near = lax.rem(row, near)
    row_far = row // near
    core = hid + 1 - 2 * lax.rem(hid, 2)
    across = lax.rem(hid + 2, 4)
    corner = lax.rem(core + 2, 4)
    mail = Mail(send, recv)
    mine = x_ref.shape[1]
    share = h0_mine.shape[1]
    mesh_rows = h0full.shape[1]
    tiles = mine // TILE
    degree = m2m_ref.shape[0]
    latent = h0_mine.shape[0]

    def peer(device):
        return {"hid": device, "rows": row}

    def row_peer(device):
        return {"hid": hid, "rows": device}

    barrier = pltpu.get_barrier_semaphore()
    for device in (core, across, corner):
        pl.semaphore_signal(barrier, inc=1, device_id=peer(device), device_id_type=MESH)
    for step in range(1, row_groups):
        pl.semaphore_signal(
            barrier,
            inc=1,
            device_id=row_peer(lax.rem(row + step, row_groups)),
            device_id_type=MESH,
        )
    pl.semaphore_wait(barrier, 3 + row_groups - 1)

    def gather_start(view):
        near_copy = mail.copy(view(hid), view(hid), peer(core))
        far_copy = mail.copy(view(hid), view(hid), peer(across))
        return near_copy, far_copy

    def gather_pass(view, copies):
        near_copy, far_copy = copies
        far_copy.wait_recv()
        return near_copy, far_copy, mail.copy(view(across), view(across), peer(core))

    def gather_wait(copies):
        near_copy, far_copy, passed = copies
        near_copy.wait_recv()
        passed.wait_recv()
        near_copy.wait_send()
        far_copy.wait_send()
        passed.wait_send()

    def rows_of(ref, block, size, start=0, width=None):
        width = ref.shape[1] if width is None else width
        return ref.at[pl.ds(pl.multiple_of(block * size, size), size), pl.ds(start, width)]

    def lanes_of(ref, block, size):
        return ref.at[:, pl.ds(pl.multiple_of(block * size, size), size)]

    w[pl.ds(pl.multiple_of(hid * 64, 64), 64), :] = wown_ref[...]
    bias[pl.ds(pl.multiple_of(hid * 64, 64), 64), :] = bown_ref[...]
    flights = {}
    for name in "gend":
        start, width = GROUPS[name]
        view = functools.partial(rows_of, w, size=64, start=start, width=width)
        flights[name] = gather_start(lambda block, view=view: view(block))
        if name == "g":
            flights["b"] = gather_start(lambda block: rows_of(bias, block, 64))

    def weights_pass(name):
        if name == "b":
            flights[name] = gather_pass(lambda block: rows_of(bias, block, 64), flights[name])
            return
        start, width = GROUPS[name]
        flights[name] = gather_pass(
            lambda block: rows_of(w, block, 64, start, width), flights[name]
        )

    lane = lax.broadcasted_iota(jnp.int32, (1, TILE), 1)
    first_row = hid * mine

    def live_mask(i):
        return (first_row + i * TILE + lane < live_ref[0]).astype(f32)

    cacc[...] = jnp.zeros_like(cacc)

    def squares(i, carry):
        here = pl.ds(pl.multiple_of(i * TILE, TILE), TILE)
        mask = live_mask(i)
        delta = (t_ref[:, here].astype(f32) - x_ref[:, here].astype(f32)) * mask
        cacc[0] += fold(delta * delta)
        cacc[1] += fold(jnp.broadcast_to(mask, (PAD, TILE)))
        return carry

    lax.fori_loop(0, tiles, squares, 0)
    col = lax.broadcasted_iota(jnp.int32, (PAD, 128), 1)
    small[...] = jnp.where(
        col == 0,
        jnp.sum(cacc[0], 1, keepdims=True),
        jnp.where(col == 1, jnp.sum(cacc[1], 1, keepdims=True), 0.0),
    )
    sum_hid = [
        mail.copy(small, sland_h.at[slot], peer(device))
        for slot, device in enumerate((core, across, corner))
    ]

    for name in "gb":
        weights_pass(name)
    gather_wait(flights["g"])
    gather_wait(flights["b"])
    b_g, b_e, b_n, b_d = (bias[:, k : k + 1] for k in range(4))
    gains = [norm_ref[:, k : k + 1] for k in range(3)]
    shifts = [norm_ref[:, k + 3 : k + 4] for k in range(3)]
    wt[:, 0:256] = flip(w[:, COLS["g2"] : COLS["g2"] + 256])
    w1g = w[:, 0:128][:, :PAD]

    def embed(inputs):
        pre = mm(w1g, inputs) + b_g
        act, slope = act_forward(pre)
        normed, scale = norm_forward(mm(wt[:, 0:256], act))
        return act, slope, normed, scale

    mesh_tmp[0] = jnp.zeros((latent, share), f32)

    def pool(i, carry):
        here = pl.ds(pl.multiple_of(i * TILE, TILE), TILE)
        mesh_tmp[0] += embed(xg_ref[:, here])[2] * gains[0] + shifts[0]
        return carry

    lax.fori_loop(0, g2m_deg, pool, 0)
    h0_mine[...] = mesh_tmp[0] * (1.0 / g2m_deg)
    my_mesh = pl.ds(pl.multiple_of(hid * share, share), share)
    h0_half = h0_mine[...].astype(bf16)
    h0full[:, my_mesh] = h0_half
    node_in[:latent, :] = h0_half
    h0_view = functools.partial(lanes_of, h0full, size=share)
    h0_flight = gather_start(lambda block: h0_view(block))

    for copy in sum_hid:
        copy.wait()
    small[...] = small[...] + sland_h[0] + sland_h[1] + sland_h[2]
    sum_rows = [
        mail.copy(small, sland_r.at[step - 1], row_peer(lax.rem(row + step, row_groups)))
        for step in range(1, row_groups)
    ]

    def own(i, carry):
        here = pl.ds(pl.multiple_of(i * TILE, TILE), TILE)
        act, slope, normed, scale = embed(x_ref[:, here])
        ds_g[:, here] = slope
        act_g[:, here] = act
        nrm_g[:, here] = normed
        scale_g[:, here] = scale
        dec_in[:latent, here] = (normed * gains[0] + shifts[0]).astype(bf16)
        return carry

    def own_range(a, b):
        lax.fori_loop(a, b, own, 0)

    own_range(0, tiles // 2)
    h0_flight = gather_pass(lambda block: h0_view(block), h0_flight)
    weights_pass("e")
    weights_pass("n")
    weights_pass("d")
    own_range(tiles // 2, tiles)
    for name in "end":
        gather_wait(flights[name])
    wt[:, 256:512] = flip(w[:, COLS["e2"] : COLS["e2"] + 256])
    wt[:, 512:768] = flip(w[:, COLS["n2"] : COLS["n2"] + 256])
    wt[:128, 768:1024] = flip(w[:, COLS["d2"] : COLS["d2"] + 128])
    gather_wait(h0_flight)

    e1 = COLS["e1"]
    mesh_tmp[0] = mm(w[:, e1 : e1 + 256], node_in[:latent, :]) + b_e
    mesh_tmp[1] = jnp.zeros((latent, share), f32)

    def edge_index(k):
        return m2m_ref[pl.ds(k, 1), my_mesh]

    def fill(index, base, rows):
        for block, part in enumerate(ones_at(index, base, rows)):
            onehot[block * 256 : block * 256 + 256, :] = part

    def edge(k, carry):
        fill(edge_index(k), 0, mesh_rows)
        sent = mm(h0full[...], onehot[...]).astype(bf16)
        hs_e[k] = sent
        pre = mesh_tmp[0] + mm(w[:, e1 + 256 : e1 + 512], sent)
        act, slope = act_forward(pre)
        act_e[k] = act
        ds_e[k] = slope
        normed, scale = norm_forward(mm(wt[:, 256:512], act))
        nrm_e[k] = normed
        scale_e[pl.ds(k, 1), :] = scale
        mesh_tmp[1] += normed * gains[1] + shifts[1]
        return carry

    lax.fori_loop(0, degree, edge, 0)

    n1 = COLS["n1"]
    node_in[latent:, :] = mesh_tmp[1].astype(bf16)
    act_n, slope_n = act_forward(mm(w[:, n1 : n1 + 512], node_in[...]) + b_n)
    normed_n, scale_n = norm_forward(mm(wt[:, 512:768], act_n))
    h1 = h0_mine[...] + (normed_n * gains[2] + shifts[2])
    ds_e[degree] = slope_n
    act_e[degree] = act_n
    nrm_e[degree] = normed_n
    scale_e[degree : degree + 1, :] = scale_n
    high, low = split2(h1)
    h1full[:latent, my_mesh] = high
    h1full[latent:, my_mesh] = low
    h1_view = functools.partial(lanes_of, h1full, size=share)
    h1_flight = gather_start(lambda block: h1_view(block))

    for copy in sum_rows:
        copy.wait()
    totals = small[...]
    for step in range(1, row_groups):
        totals = totals + sland_r[step - 1]
    tot_ref[...] = totals
    count = totals[:, 1:2]
    var = totals[:, 0:1] / count + 1e-06
    d_bias = chan_ref[:, 0:1]
    level = chan_ref[:, 1:2]
    loss_weight = count * jnp.sum(level, 0, keepdims=True)
    weight_var = level / var
    pull = 2.0 * weight_var / loss_weight
    nacc[...] = jnp.zeros_like(nacc)
    bacc[...] = jnp.zeros_like(bacc)
    cacc[...] = jnp.zeros_like(cacc)
    grad[...] = jnp.zeros_like(grad)
    dsum[...] = jnp.zeros_like(dsum)

    h1_flight = gather_pass(lambda block: h1_view(block), h1_flight)
    gather_wait(h1_flight)

    d1, d2 = COLS["d1"], COLS["d2"]
    my_grid = hid * mine

    def decode(i, carry):
        here = pl.ds(pl.multiple_of(i * TILE, TILE), TILE)
        fill(m2g_ref[:, pl.ds(pl.multiple_of(my_grid + i * TILE, TILE), TILE)], 0, mesh_rows)
        both = mm(h1full[...], onehot[...])
        back = (both[:latent] + both[latent:]) * (1.0 / m2g_deg)
        dec_in[latent:, here] = back.astype(bf16)
        pre = mm(w[:, d1 : d1 + 512], dec_in[:, here]) + b_d
        act, slope = act_forward(pre)
        out = mm(wt[:128, 768:1024], act)[:PAD]
        err = x_ref[:, here].astype(f32) + out + d_bias - t_ref[:, here].astype(f32)
        kept = err * live_mask(i)
        cacc[1] += fold(weight_var * kept * err)
        pred_grad = pull * kept
        cacc[0] += fold(pred_grad)
        upstream = pred_grad.astype(bf16)
        act_grad = mm(w[:, d2 : d2 + 128][:, :PAD], upstream)
        pre_grad = (act_grad * slope).astype(bf16)
        dp_d[:, here] = pre_grad
        dsum[...] += mt(pre_grad, onehot[...])
        grad[:, d2 : d2 + PAD] += mt(act, upstream)
        return carry

    lax.fori_loop(0, tiles, decode, 0)

    def spread_start(view, land):
        return (
            mail.copy(view(corner), land.at[1], peer(core)),
            mail.copy(view(core), land.at[0], peer(core)),
        )

    def spread_across(view, land, land_far, copies):
        copies[0].wait()
        view(across)[...] = view(across)[...] + land[1]
        return copies + (mail.copy(view(across), land_far, peer(across)),)

    def spread_end(view, land, land_far, copies):
        copies[1].wait()
        copies[2].wait()
        return view(hid)[...] + land[0] + land_far[...]

    d_view = functools.partial(lanes_of, dsum, size=share)

    def view_d(block):
        return d_view(block)

    d_flight = spread_start(view_d, land_a.at[0])
    w1d_low = flip(w[:, d1 : d1 + 256])
    wt[:, 1024:1280] = w1d_low
    d_flight = spread_across(view_d, land_a.at[0], land_b.at[0], d_flight)

    def decode_rest(i, carry):
        here = pl.ds(pl.multiple_of(i * TILE, TILE), TILE)
        pre_grad = dp_d[:, here]
        dglat[:, here] = mm(wt[:, 1024:1280], pre_grad)
        grad[:, d1 : d1 + 512] += mt(pre_grad, dec_in[:, here])
        bacc[3] += fold(pre_grad.astype(f32))
        return carry

    lax.fori_loop(0, tiles, decode_rest, 0)
    wt[:, 1024:1280] = flip(w[:, d1 + 256 : d1 + 512])
    wt[:, 1280:1536] = flip(w[:, n1 : n1 + 256])
    wt[:, 1536:1792] = flip(w[:, n1 + 256 : n1 + 512])
    wt[:, 1792:2048] = flip(w[:, e1 : e1 + 256])
    wt[:, 2048:2304] = flip(w[:, e1 + 256 : e1 + 512])

    high, low = split2(spread_end(view_d, land_a.at[0], land_b.at[0], d_flight))
    h1_grad = (mm(wt[:, 1024:1280], high) + mm(wt[:, 1024:1280], low)) * (1.0 / m2g_deg)
    nacc[2] += fold(h1_grad * nrm_e[degree])
    nacc[5] += fold(h1_grad)
    up_n = norm_backward(
        h1_grad, nrm_e[degree], scale_e[degree : degree + 1, :], gains[2]
    ).astype(bf16)
    n2 = COLS["n2"]
    pre_grad_n = (mm(w[:, n2 : n2 + 256], up_n) * ds_e[degree]).astype(bf16)
    mesh_tmp[0] = h1_grad + mm(wt[:, 1280:1536], pre_grad_n)
    mesh_tmp[1] = mm(wt[:, 1536:1792], pre_grad_n)

    dsum[...] = jnp.zeros_like(dsum)
    e2 = COLS["e2"]

    def edge_back(k, carry):
        upstream = mesh_tmp[1]
        normed = nrm_e[k]
        nacc[1] += fold(upstream * normed)
        nacc[4] += fold(upstream)
        up = norm_backward(upstream, normed, scale_e[pl.ds(k, 1), :], gains[1]).astype(bf16)
        pre_grad = (mm(w[:, e2 : e2 + 256], up) * ds_e[k]).astype(bf16)
        fill(edge_index(k), 0, mesh_rows)
        dsum[...] += mt(pre_grad, onehot[...])
        mesh_tmp[0] += mm(wt[:, 1792:2048], pre_grad)
        grad[:, e2 : e2 + 256] += mt(act_e[k], up)
        grad[:, e1 : e1 + 256] += mt(pre_grad, node_in[:latent, :])
        grad[:, e1 + 256 : e1 + 512] += mt(pre_grad, hs_e[k])
        bacc[1] += fold(pre_grad.astype(f32))
        return carry

    lax.fori_loop(0, degree, edge_back, 0)
    e_flight = spread_start(view_d, land_a.at[1])
    grad[:, n2 : n2 + 256] = mt(act_e[degree], up_n)
    e_flight = spread_across(view_d, land_a.at[1], land_b.at[1], e_flight)
    grad[:, n1 : n1 + 512] = mt(pre_grad_n, node_in[...])
    bacc[2] += fold(pre_grad_n.astype(f32))
    high, low = split2(spread_end(view_d, land_a.at[1], land_b.at[1], e_flight))
    h0_grad = mesh_tmp[0] + mm(wt[:, 2048:2304], high) + mm(wt[:, 2048:2304], low)
    high, low = split2(h0_grad * (1.0 / g2m_deg))
    hgfull[:latent, my_mesh] = high
    hgfull[latent:, my_mesh] = low
    hg_view = functools.partial(lanes_of, hgfull, size=share)
    hg_flight = gather_start(lambda block: hg_view(block))

    def chunk(start, width, block):
        return rows_of(grad, block, 64, start, width)

    def reduce_start(name):
        start, width = GROUPS[name]
        flight = (
            mail.copy(
                chunk(start, width, corner), gland_a.at[1, :, pl.ds(start, width)], peer(core)
            ),
            mail.copy(
                chunk(start, width, core), gland_a.at[0, :, pl.ds(start, width)], peer(core)
            ),
        )
        return flight

    def reduce_across(name, flight):
        start, width = GROUPS[name]
        cols = pl.ds(start, width)
        flight[0].wait()
        view = chunk(start, width, across)
        view[...] = view[...] + gland_a[1, :, cols]
        return flight + (mail.copy(view, gland_b.at[:, cols], peer(across)),)

    def reduce_rows(name, flight):
        start, width = GROUPS[name]
        cols = pl.ds(start, width)
        flight[1].wait()
        flight[2].wait()
        part = 64 // near
        held[:, cols] = chunk(start, width, hid)[...] + gland_a[0, :, cols] + gland_b[:, cols]
        copies = []
        for step in range(1, near):
            to = lax.rem(row_near + step, near)
            copies.append(
                mail.copy(
                    held.at[pl.ds(pl.multiple_of(to * part, part), part), cols],
                    rland.at[step - 1, :, cols],
                    row_peer(row_far * near + to),
                )
            )
        return copies

    def reduce_share(name, copies):
        start, width = GROUPS[name]
        cols = pl.ds(start, width)
        part = 64 // near
        own_rows = pl.ds(pl.multiple_of(row_near * part, part), part)
        own_part = out_ref.at[own_rows, cols]
        for copy in copies:
            copy.wait()
        total = held[own_rows, cols]
        for step in range(1, near):
            total = total + rland[step - 1, :, cols]
        if far > 1:
            fland[far - 1, :, cols] = total
            more = []
            for step in range(1, far):
                to = lax.rem(row_far + step, far)
                more.append(
                    mail.copy(
                        fland.at[far - 1, :, cols],
                        fland.at[step - 1, :, cols],
                        row_peer(to * near + row_near),
                    )
                )
            for copy in more:
                copy.wait()
            total = fland[far - 1, :, cols]
            for step in range(1, far):
                total = total + fland[step - 1, :, cols]
        own_part[...] = total
        out = []
        for step in range(1, near):
            to = lax.rem(row_near + step, near)
            out.append(mail.copy(own_part, own_part, row_peer(row_far * near + to)))
        return out

    hg_flight = gather_pass(lambda block: hg_view(block), hg_flight)
    gather_wait(hg_flight)

    def grid_back(i, carry):
        here = pl.ds(pl.multiple_of(i * TILE, TILE), TILE)
        base = my_grid + i * TILE
        both = None
        for at in range(0, mesh_rows, TILE):
            parts = ones_at(g2m_ref[:, at : at + TILE], base, TILE)
            for block, part in enumerate(parts):
                onehot[block * 256 + 0 : block * 256 + 256, :] = part
            term = mt(hgfull[:, at : at + TILE], onehot[:TILE, :])
            both = term if both is None else both + term
        upstream = dglat[:, here] + both[:latent] + both[latent:]
        normed = nrm_g[:, here]
        nacc[0] += fold(upstream * normed)
        nacc[3] += fold(upstream)
        up = norm_backward(upstream, normed, scale_g[:, here], gains[0]).astype(bf16)
        pre_grad = (mm(w[:, COLS["g2"] : COLS["g2"] + 256], up) * ds_g[:, here]).astype(bf16)
        grad[:, COLS["g2"] : COLS["g2"] + 256] += mt(act_g[:, here], up)
        grad[:, 0:PAD] += mt(pre_grad, x_ref[:, here])
        bacc[0] += fold(pre_grad.astype(f32))
        return carry

    lax.fori_loop(0, tiles, grid_back, 0)

    narrow = grad[:, 0:128]
    at_col = lax.broadcasted_iota(jnp.int32, (latent, 128), 1)
    for k in range(4):
        narrow = jnp.where(at_col == PAD + k, jnp.sum(bacc[k], 1, keepdims=True), narrow)
    for k in range(6):
        narrow = jnp.where(at_col == 96 + k, jnp.sum(nacc[k], 1, keepdims=True), narrow)
    grad[:, 0:128] = narrow
    side = grad[:PAD, 0:128]
    for k in range(2):
        side = jnp.where(col == 102 + k, jnp.sum(cacc[k], 1, keepdims=True), side)
    grad[:PAD, 0:128] = side

    names = "dneg"
    stage = {name: reduce_start(name) for name in names}
    stage = {name: reduce_across(name, stage[name]) for name in names}
    stage = {name: reduce_rows(name, stage[name]) for name in names}
    stage = {name: reduce_share(name, stage[name]) for name in names}
    for name in names:
        for copy in stage[name]:
            copy.wait()
    all_ref[pl.ds(pl.multiple_of(hid * 64, 64), 64), :] = out_ref[:, 0:128]
    last = [
        mail.copy(rows_of(all_ref, hid, 64), rows_of(all_ref, hid, 64), peer(device))
        for device in (core, across, corner)
    ]
    for copy in last:
        copy.wait()


def adam_step(weight, avg, sq, grad, rate, decay):
    avg_new = 0.5 * avg + 0.5 * grad
    sq_new = 0.5 * sq + 0.5 * grad * grad
    fix = 1.0 - 0.5**STEP_COUNT
    step = avg_new / fix / (jnp.sqrt(sq_new / fix) + 1e-08)
    return (weight - rate * (step + decay * weight), avg_new, sq_new)


def adam_kernel(out_ref, all_ref, *refs):
    ins, outs = refs[:21], refs[21:]

    def update(array, at, grad, rate, decay):
        fresh, avg_new, sq_new = adam_step(
            ins[array][at], ins[7 + array][at], ins[14 + array][at], grad, rate, decay
        )
        outs[array][at] = fresh
        outs[7 + array][at] = avg_new
        outs[14 + array][at] = sq_new
        if array < 4:
            outs[21 + array][at] = fresh.astype(bf16)

    everything = (slice(None), slice(None))
    channels = ins[0].shape[1]
    update(0, everything, out_ref[:, 0:128][:, :channels], 0.05, 0.1)
    for layer, name in enumerate(("e1", "n1", "d1")):
        update(1, (layer,) + everything, out_ref[:, COLS[name] : COLS[name] + 512], 0.05, 0.1)
    for layer, name in enumerate(("g2", "e2", "n2")):
        update(2, (layer,) + everything, out_ref[:, COLS[name] : COLS[name] + 256], 0.05, 0.1)
    update(3, everything, out_ref[:, COLS["d2"] : COLS["d2"] + 128][:, :channels], 0.05, 0.1)
    turned = out_ref[:, 0:128].T
    update(4, everything, turned[PAD : PAD + 4, :], 0.3, 0.0)
    wide = all_ref[...].T
    update(5, everything, wide[96:102, :], 0.3, 0.0)
    update(6, everything, wide[102:103, :128], 0.3, 0.0)


def body(
    grid_input,
    grid_target,
    live_points,
    level_weight,
    g2m_index,
    m2m_index,
    m2g_index,
    *params,
):
    groups = lax.axis_size("hid")
    row_groups = lax.axis_size("rows")
    place = lax.axis_index("hid")
    masters, avgs, squares = params[:7], params[7:14], params[14:21]
    grid_first, wide_first, second_layer, decode_second, hidden_bias, norm_params, decode_bias = (
        masters
    )
    grid_rows, channels = grid_input.shape
    mesh_rows, degree = m2m_index.shape
    latent = norm_params.shape[2]
    share = mesh_rows // groups
    mine = grid_rows // groups
    g2m_deg = g2m_index.shape[1]
    m2g_deg = m2g_index.shape[1]
    whole = pl.BlockSpec(memory_space=pltpu.VMEM)
    scalar = pl.BlockSpec(memory_space=pltpu.SMEM)

    g2m = g2m_index.T
    xm, tm, xg = pl.pallas_call(
        pick_kernel,
        out_shape=[jax.ShapeDtypeStruct((PAD, mine), bf16)] * 2
        + [jax.ShapeDtypeStruct((PAD, g2m_deg * share), bf16)],
        in_specs=[scalar, scalar, whole, whole],
        out_specs=[whole] * 3,
        scratch_shapes=[
            pltpu.VMEM((grid_rows, 128), f32),
            pltpu.VMEM((g2m_deg * share, 128), f32),
        ],
        compiler_params=pltpu.CompilerParams(vmem_limit_bytes=48 * 2**20),
        name="pick",
    )(
        place[None].astype(jnp.int32),
        lax.dynamic_slice_in_dim(g2m, place * share, share, 1),
        grid_input.T,
        grid_target.T,
    )

    def half(values, width):
        values = values.astype(bf16)
        return jnp.pad(values, ((0, 0), (0, width - values.shape[1])))

    wide_t = wide_first.transpose(0, 2, 1)
    pack = jnp.concatenate(
        [
            half(grid_first.T, 128),
            half(second_layer[0], 256),
            half(wide_t[0], 512),
            half(second_layer[1], 256),
            half(wide_t[1], 512),
            half(second_layer[2], 256),
            half(wide_t[2], 512),
            half(decode_second, 128),
        ],
        1,
    )
    bias_cols = jnp.pad(hidden_bias.T, ((0, 0), (0, 124)))
    norm_cols = jnp.pad(norm_params.reshape(6, latent).T, ((0, 0), (0, 122)))
    chan_cols = jnp.pad(
        jnp.stack([decode_bias, level_weight.astype(f32)], 1), ((0, PAD - channels), (0, 126))
    )
    copies = count_copies(row_groups)
    near = min(row_groups, 8)
    far = row_groups // near
    summed, spare, totals = pl.pallas_call(
        functools.partial(
            main_kernel, row_groups=row_groups, g2m_deg=g2m_deg, m2g_deg=m2g_deg
        ),
        out_shape=[
            jax.ShapeDtypeStruct((64, PACK), f32),
            jax.ShapeDtypeStruct((256, 128), f32),
            jax.ShapeDtypeStruct((PAD, 128), f32),
        ],
        in_specs=[scalar] + [whole] * 10,
        out_specs=[whole] * 3,
        scratch_shapes=[
            pltpu.VMEM((256, PACK), bf16),
            pltpu.VMEM((256, 2304), bf16),
            pltpu.VMEM((256, 128), f32),
            pltpu.VMEM((latent, mesh_rows), bf16),
            pltpu.VMEM((2 * latent, mesh_rows), bf16),
            pltpu.VMEM((2 * latent, mesh_rows), bf16),
            pltpu.VMEM((mesh_rows, TILE), bf16),
            pltpu.VMEM((latent, mine), f32),
            pltpu.VMEM((latent, mine), bf16),
            pltpu.VMEM((latent, mine), f32),
            pltpu.VMEM((1, mine), f32),
            pltpu.VMEM((2 * latent, mine), bf16),
            pltpu.VMEM((latent, mine), bf16),
            pltpu.VMEM((latent, mine), f32),
            pltpu.VMEM((degree + 1, latent, share), f32),
            pltpu.VMEM((degree + 1, latent, share), bf16),
            pltpu.VMEM((degree, latent, share), bf16),
            pltpu.VMEM((degree + 1, latent, share), f32),
            pltpu.VMEM((8, share), f32),
            pltpu.VMEM((latent, mesh_rows), f32),
            pltpu.VMEM((2, 2, latent, share), f32),
            pltpu.VMEM((2, latent, share), f32),
            pltpu.VMEM((256, PACK), f32),
            pltpu.VMEM((2, 64, PACK), f32),
            pltpu.VMEM((64, PACK), f32),
            pltpu.VMEM((64, PACK), f32),
            pltpu.VMEM((near - 1, 64 // near, PACK), f32),
            pltpu.VMEM((far, 64 // near, PACK), f32),
            pltpu.VMEM((6, latent, 128), f32),
            pltpu.VMEM((4, latent, 128), f32),
            pltpu.VMEM((2, PAD, 128), f32),
            pltpu.VMEM((latent, share), f32),
            pltpu.VMEM((2 * latent, share), bf16),
            pltpu.VMEM((2, latent, share), f32),
            pltpu.VMEM((PAD, 128), f32),
            pltpu.VMEM((3, PAD, 128), f32),
            pltpu.VMEM((row_groups - 1, PAD, 128), f32),
            pltpu.SemaphoreType.DMA((copies,)),
            pltpu.SemaphoreType.DMA((copies,)),
        ],
        compiler_params=pltpu.CompilerParams(
            collective_id=0, has_side_effects=True, vmem_limit_bytes=64 * 2**20
        ),
        name="step",
    )(
        live_points,
        xm,
        tm,
        xg,
        g2m,
        m2m_index.T,
        m2g_index.T,
        pack,
        bias_cols,
        norm_cols,
        chan_cols,
    )

    def flat(arrays):
        first, wide, second, last, bias, norm, out_bias = arrays
        return (
            first.T,
            wide.transpose(0, 2, 1),
            second,
            last,
            bias,
            norm.reshape(6, latent),
            jnp.pad(out_bias[None], ((0, 0), (0, 128 - channels))),
        )

    def unflat(arrays):
        first, wide, second, last, bias, norm, out_bias = arrays
        return (
            first.T,
            wide.transpose(0, 2, 1),
            second,
            last,
            bias,
            norm.reshape(2, 3, latent),
            out_bias[0, :channels],
        )

    operands = flat(masters) + flat(avgs) + flat(squares)
    shapes = [jax.ShapeDtypeStruct(v.shape, f32) for v in operands]
    shapes += [jax.ShapeDtypeStruct(v.shape, bf16) for v in operands[:4]]
    outs = pl.pallas_call(
        adam_kernel,
        out_shape=shapes,
        in_specs=[whole] * 23,
        out_specs=[whole] * 25,
        compiler_params=pltpu.CompilerParams(vmem_limit_bytes=32 * 2**20),
        name="adam",
    )(summed, spare, *operands)
    halves = outs[21:]
    loss_total = jnp.sum(spare[:PAD, 103])
    loss_weight = totals[0, 1] * jnp.sum(level_weight.astype(f32))
    return (
        (loss_total, loss_weight)
        + unflat(outs[0:7])
        + unflat(outs[7:14])
        + unflat(outs[14:21])
        + (halves[0].T, halves[1].transpose(0, 2, 1), halves[2], halves[3])
    )


def solution(mesh):
    weights = (
        P(None, "hid"),
        P(None, None, "hid"),
        P(None, "hid", None),
        P("hid", None),
        P(None, "hid"),
        P(),
        P(),
    )
    in_specs = (
        P("rows", None),
        P("rows", None),
        P("rows"),
        P(),
        P("rows", None),
        P("rows", None),
        P("rows", None),
    ) + weights * 3
    out_specs = (P(), P()) + weights * 3 + weights[:4]
    return jax.shard_map(body, mesh=mesh, in_specs=in_specs, out_specs=out_specs, check_vma=False)
```

time: 2240 us -> 259 us (0.12)
  waiting for transfers between devices: 1150 us -> 0 us
  local copies, waits for them, and re-layouts: 501 us -> 35.4 us
  other arithmetic: 323 us -> 5.56 us
  Pallas kernels: 0 us -> 213 us
  blocking collectives: 118 us -> 0 us
  matrix products: 112 us -> 0 us
    reduce_scatter x10 -> x0, waiting for transfers between devices: 909 us -> none  [the longest x3 456 us: input_share(): return lax.psum_scatter(input_part, 'hid', scatter_dimension=0, tiled=True)]
    gather x5 -> x0, local copies, waits for them, and re-layouts: 387 us -> none  [the longest x2 259 us: body(): back = jnp.mean(h1[m2g_index], 1)]
    pallas_call x0 -> x3, Pallas kernels: none -> 213 us  [the longest x1 195 us: body(): pl.pallas_call(functools.partial(main_kernel, row_groups=row_groups, g2m_...]
    all_gather x7 -> x0, waiting for transfers between devices: 210 us -> none  [the longest x3 121 us: gather_rows(): return lax.all_gather(values, 'hid', axis=0, tiled=True)]
    reduce_sum x18 -> x2, other arithmetic: 147 us -> 2.07 us  [the longest x1 1.46 us: body(): loss_total = jnp.sum(spare[:PAD, 103])]
    psum x3 -> x0, blocking collectives: 118 us -> none  [the longest x1 40.1 us: body(): lax.psum((norm_grad, jnp.sum(pred_grad, 0), local_loss), ('rows', 'hid'))]
    scatter-add x3 -> x0, other arithmetic: 116 us -> none  [graph_sum(): whole = jax.ops.segment_sum(values, targets, num_segments=count)]
    dot_general x23 -> x0, matrix products: 112 us -> none  [the longest x15 70.8 us: contract(): lax.dot_general(left, right, (((left_dim,), (right_dim,)), ((), ())), pre...]
  transfers between devices with their start and end apart: 18 -> 0, of which waited for: 17 -> 0; matrix products, arithmetic and copies ran while one was open for 3% -> 0% of each run, Pallas kernels for 0% -> 0%
where the time goes in v1:
time: 259 us; the launch traced here: 258 us
  Pallas kernels  213 us (82%)
  local copies, waits for them, and re-layouts  35.4 us (14%)
  other arithmetic  5.56 us (2%)
  between operations  3.77 us (1%)
    pallas_call x1, Pallas kernels, body(): pl.pallas_call(functools.partial(main_kernel, row_groups=row_groups, g2m_...  195 us
    unnamed x70, local copies, waits for them, and re-layouts  27.6 us
    pallas_call x1, Pallas kernels, body(): pl.pallas_call(pick_kernel, out_shape=[jax.ShapeDtypeStruct((PAD, mine),...  15.7 us

profile of v1, /device:TPU:0, one launch (start us, length us, event | category | flops | bytes accessed | tf_op | source)
XLA Modules:
  0.0 257.5 jit_solution(7527110196520368883)
XLA Ops:
  0.7 0.9 convert.10
  1.6 0.8 bitcast_convert_fusion.1
  2.4 0.6 constant_dynamic-update-slice_fusion.1
  3.0 0.6 fusion.5
  3.6 1.0 bitcast_convert_fusion
  4.6 0.6 fusion.2
  5.3 0.6 fusion.4
  5.9 0.6 fusion.1
  6.5 0.6 fusion.3
  7.1 0.6 fusion
  7.8 0.8 convert_element_type.54
  8.5 0.6 constant_dynamic-update-slice_fusion.wown_ref
  9.1 0.7 dynamic-slice_bitcast_fusion.index_ref
  9.9 1.7 copy-done
  11.6 15.7 %pick.1 = (bf16[80,4096]{1,0:T(8,128)(2,1)S(1)}, bf16[80,4096]{1,0:T(8,128)(2,1)S(1)}, bf16[80,4096]{1,0:T(8,128)(2,1)S(1)}) custom-call(s32[1]{0:T(128)} %bitcast.place_ref, s32[8,512]{1,0:T(8,128)S(1)} %dynamic-slice_bitcast_fusion.index_ref, bf16[78,16384]{1,0:T(8,128)(2,1)S(1)} %bitcast.63, bf16[78,16384]{1,0:T(8,128)(2,1)} %bitcast.70), custom_call_target="tpu_custom_call" | custom-call | tf_op jit(solution)/shard_map/pick/pallas_call | solution.py:761
  27.3 0.8 copy-done.4
  28.2 0.9 copy-done.5
  29.1 0.9 copy-done.6
  30.7 0.7 pad.32.norm_ref
  31.5 0.6 pad.33.chan_ref
  32.2 0.6 pad.31.bown_ref
  33.5 195.2 %step.1 = (f32[64,2560]{1,0:T(8,128)}, f32[256,128]{1,0:T(8,128)}, f32[80,128]{1,0:T(8,128)}) custom-call(s32[1]{0:T(128)S(6)} %copy.91.live_ref, bf16[80,4096]{1,0:T(8,128)(2,1)} %copy-done.4, bf16[80,4096]{1,0:T(8,128)(2,1)} %copy-done.5, bf16[80,4096]{1,0:T(8,128)(2,1)} %copy-done.6, s32[8,2048]{1,0:T(8,128)} %bitcast.74, s32[6,2048]{1,0:T(8,128)} %bitcast.75, ...), custom_call_target="tpu_custom_call" | custom-call | tf_op jit(solution)/shard_map/step/pallas_call | solution.py:806
  228.7 0.7 copy.79
  229.4 0.7 copy.80
  230.1 0.7 pad.34.refs_6_
  230.8 0.7 pad.35.refs_13_
  231.5 0.7 pad.36.refs_20_
  232.1 1.0 copy-done.1
  233.1 0.9 copy-done.2
  234.0 1.1 copy-done.3
  235.1 1.0 copy-done.7
  236.1 1.0 copy-done.8
  237.1 0.9 copy-done.9
  238.0 0.9 copy-done.10
  239.0 0.9 copy-done.11
  239.9 0.8 copy-done.12
  240.6 0.8 copy-done.13
  241.4 0.7 copy-done.15
  242.1 0.8 copy-done.16
  242.9 0.8 copy-done.17
  243.6 0.8 copy-done.18
  244.4 0.8 copy-done.19
  245.1 0.7 copy-done.21
  245.8 0.7 copy-done.22
  246.5 0.7 copy-done.23
  247.2 1.8 adam.1
  251.9 1.5 slice_reduce_fusion
  253.3 1.3 slice.46
  (52 shorter events, 4.5 us)
Async XLA Ops:
  9.9 1.7 copy-start
  11.6 18.3 %copy-start.24 = (f32[2,3,256]{2,0,1:T(2,128)S(1)}, f32[2,3,256]{2,0,1:T(2,128)}, u32[]{:S(2)}) copy-start(f32[2,3,256]{2,0,1:T(2,128)} %param.40) | copy-start | bytes 18436
  11.6 19.7 %copy-start.26 = (s32[78]{0:T(128)S(1)}, s32[78]{0:T(128)}, u32[]{:S(2)}) copy-start(s32[78]{0:T(128)} %param.31) | copy-start | bytes 940
  11.6 19.7 %copy-start.25 = (f32[78]{0:T(128)S(1)}, f32[78]{0:T(128)}, u32[]{:S(2)}) copy-start(f32[78]{0:T(128)} %param.41) | copy-start | bytes 940
  11.6 20.5 %copy-start.20 = (f32[4,64]{1,0:T(4,128)S(1)}, f32[4,64]{1,0:T(4,128)}, u32[]{:S(2)}) copy-start(f32[4,64]{1,0:T(4,128)} %refs_4_.1) | copy-start | bytes 3076
  27.3 0.9 copy-start.4
  28.2 0.9 copy-start.5
  29.1 0.9 copy-start.6
  30.1 0.6 copy-start.14
  228.7 25.9 %copy-start.27 = (s32[78]{0:T(128)S(1)}, s32[78]{0:T(128)}, u32[]{:S(2)}) copy-start(s32[78]{0:T(128)} %param.31) | copy-start | bytes 940
  232.1 1.0 copy-start.1
  233.1 0.9 copy-start.2
  234.0 1.1 copy-start.3
  235.1 1.0 copy-start.7
  236.1 1.0 copy-start.8
  237.1 0.9 copy-start.9
  238.0 0.9 copy-start.10
  239.0 0.9 copy-start.11
  239.9 0.8 copy-start.12
  240.6 0.8 copy-start.13
  241.4 0.7 copy-start.15
  242.1 0.8 copy-start.16
  242.9 0.8 copy-start.17
  243.6 0.8 copy-start.18
  244.4 0.8 copy-start.19
  245.1 0.7 copy-start.21
  245.8 0.7 copy-start.22
  246.5 0.7 copy-start.23

commit v2 on v1

v2 whole, which is shorter than its diff:
```python
import functools

import jax
import jax.numpy as jnp
from jax import lax
from jax.experimental import pallas as pl
from jax.experimental.pallas import tpu as pltpu
from jax.sharding import PartitionSpec as P

STEP_COUNT = 5
MESH = pl.DeviceIdType.MESH
bf16 = jnp.bfloat16
f32 = jnp.float32
TILE = 512
PAD = 80
COLS = {"g1": 0, "g2": 128, "e1": 384, "e2": 896, "n1": 1152, "n2": 1664, "d1": 1920, "d2": 2432}
GROUPS = {"g": (0, 384), "e": (384, 768), "n": (1152, 768), "d": (1920, 640)}
PACK = 2560


def mm(left, right):
    return lax.dot_general(left, right, (((1,), (0,)), ((), ())), preferred_element_type=f32)


def mt(left, right):
    return lax.dot_general(left, right, (((1,), (1,)), ((), ())), preferred_element_type=f32)


def flip(values):
    return values.astype(f32).T.astype(bf16)


def split2(values):
    high = values.astype(bf16)
    low = (values - high.astype(f32)).astype(bf16)
    return high, low


def fold(values):
    total = values[:, :128]
    for at in range(128, values.shape[1], 128):
        total = total + values[:, at : at + 128]
    return total


def ones_at(index, base, rows):
    lanes = index.shape[1]
    local = lax.broadcasted_iota(jnp.int32, (256, lanes), 0).astype(f32).astype(bf16)
    parts = []
    for block in range(rows // 256):
        total = None
        for k in range(index.shape[0]):
            shifted = (index[k : k + 1] - (base + block * 256)).astype(f32).astype(bf16)
            hit = jnp.where(
                jnp.broadcast_to(shifted, (256, lanes)) == local,
                jnp.asarray(1, bf16),
                jnp.asarray(0, bf16),
            )
            total = hit if total is None else total + hit
        parts.append(total)
    return parts


def act_forward(pre):
    sigma = 0.5 * jnp.tanh(0.5 * pre) + 0.5
    act = pre * sigma
    return act.astype(bf16), sigma + act * (1.0 - sigma)


def norm_forward(values):
    size = values.shape[0]
    centre = values - jnp.sum(values, 0, keepdims=True) * (1.0 / size)
    var = jnp.sum(centre * centre, 0, keepdims=True) * (1.0 / size)
    scale = lax.rsqrt(var + 1e-05)
    return centre * scale, scale


def norm_backward(upstream, normed, scale, gain):
    size = upstream.shape[0]
    scaled = upstream * gain
    first = jnp.sum(scaled, 0, keepdims=True) * (1.0 / size)
    second = jnp.sum(scaled * normed, 0, keepdims=True) * (1.0 / size)
    return scale * (scaled - first - normed * second)


class Mail:
    def __init__(self, send, recv):
        self.send, self.recv, self.used = send, recv, 0

    def copy(self, source, target, device):
        at = self.used
        self.used += 1
        if self.send is None:
            return None
        copy = pltpu.make_async_remote_copy(
            src_ref=source,
            dst_ref=target,
            send_sem=self.send.at[at],
            recv_sem=self.recv.at[at],
            device_id=device,
            device_id_type=MESH,
        )
        copy.start()
        return copy


def count_copies(row_groups):
    near = min(row_groups, 8)
    far = row_groups // near
    sums = 3 + (row_groups - 1)
    rows_sum = 2 * (near - 1) + (far - 1)
    return 15 + 9 + 6 + 2 * sums + 4 * (3 + rows_sum)


def put(ref, at, values):
    for c in range(0, TILE, 128):
        ref[pl.ds(pl.multiple_of(at + 2 * c, 256), 256), :] = values[:, c : c + 128]


def take(ref, at):
    return jnp.concatenate(
        [ref[pl.ds(pl.multiple_of(at + 2 * c, 256), 256), :] for c in range(0, TILE, 128)], 1
    )


def main_kernel(
    live_ref,
    pick_ref,
    xt_hbm,
    tt_hbm,
    g2m_hbm,
    m2m_hbm,
    m2g_hbm,
    first_hbm,
    wide_hbm,
    second_hbm,
    last_hbm,
    hbias_hbm,
    norm_hbm,
    dbias_hbm,
    level_hbm,
    out_ref,
    all_ref,
    tot_ref,
    xt,
    tt,
    g2m_ref,
    m2m_ref,
    m2g_ref,
    first_f,
    last_f,
    hbias_f,
    norm_f,
    dbias_f,
    level_f,
    local_sem,
    square_tmp,
    norm_ref,
    chan_ref,
    big,
    x_ref,
    w,
    wt,
    bias,
    h0full,
    h1full,
    hgfull,
    onehot,
    spots,
    act_g,
    scale_g,
    dec_in,
    dp_d,
    ds_e,
    act_e,
    hs_e,
    nrm_e,
    scale_e,
    dsum,
    land_a,
    land_b,
    half_out,
    grad,
    gland_a,
    gland_b,
    held,
    rland,
    fland,
    nacc,
    cacc,
    h0_mine,
    node_in,
    mesh_tmp,
    small,
    sland_h,
    sland_r,
    narrow,
    nland_h,
    nland_r,
    send,
    recv,
    *,
    row_groups,
    g2m_deg,
    m2g_deg,
):
    hid = lax.axis_index("hid")
    row = lax.axis_index("rows")
    near = min(row_groups, 8)
    far = row_groups // near
    row_near = lax.rem(row, near)
    row_far = row // near
    core = hid + 1 - 2 * lax.rem(hid, 2)
    across = lax.rem(hid + 2, 4)
    corner = lax.rem(core + 2, 4)
    mail = Mail(send, recv)
    channels, grid_rows = xt.shape
    mine = x_ref.shape[1]
    share = h0_mine.shape[1]
    mesh_rows = h0full.shape[1]
    tiles = mine // TILE
    degree = m2m_ref.shape[0]
    latent = h0_mine.shape[0]

    def peer(device):
        return {"hid": device, "rows": row}

    def row_peer(device):
        return {"hid": hid, "rows": device}

    barrier = pltpu.get_barrier_semaphore()
    for device in (core, across, corner):
        pl.semaphore_signal(barrier, inc=1, device_id=peer(device), device_id_type=MESH)
    for step in range(1, row_groups):
        pl.semaphore_signal(
            barrier,
            inc=1,
            device_id=row_peer(lax.rem(row + step, row_groups)),
            device_id_type=MESH,
        )

    my_grid = pl.multiple_of(hid * mine, mine)
    pairs = (
        (first_hbm, first_f),
        (hbias_hbm, hbias_f),
        *((second_hbm.at[k], gland_a.at[1, :, pl.ds(256 * k, 256)]) for k in range(3)),
        *((wide_hbm.at[k], gland_a.at[0, :, pl.ds(512 * k, 512)]) for k in range(3)),
        (last_hbm, last_f),
        (xt_hbm, xt),
        (norm_hbm, norm_f),
        (dbias_hbm, dbias_f),
        (level_hbm, level_f),
        (tt_hbm.at[:, pl.ds(my_grid, mine)], tt),
        (m2m_hbm, m2m_ref),
        (m2g_hbm.at[:, pl.ds(my_grid, mine)], m2g_ref),
        (g2m_hbm, g2m_ref),
    )
    fetches = [
        pltpu.make_async_copy(source, target, local_sem.at[at])
        for at, (source, target) in enumerate(pairs)
    ]
    for fetch in fetches:
        fetch.start()

    def gather_start(view):
        near_copy = mail.copy(view(hid), view(hid), peer(core))
        far_copy = mail.copy(view(hid), view(hid), peer(across))
        return near_copy, far_copy

    def gather_pass(view, copies):
        near_copy, far_copy = copies
        far_copy.wait_recv()
        return near_copy, far_copy, mail.copy(view(across), view(across), peer(core))

    def gather_wait(copies):
        near_copy, far_copy, passed = copies
        near_copy.wait_recv()
        passed.wait_recv()
        near_copy.wait_send()
        far_copy.wait_send()
        passed.wait_send()

    def rows_of(ref, block, size, start=0, width=None):
        width = ref.shape[1] if width is None else width
        return ref.at[pl.ds(pl.multiple_of(block * size, size), size), pl.ds(start, width)]

    def lanes_of(ref, block, size):
        return ref.at[:, pl.ds(pl.multiple_of(block * size, size), size)]

    own_rows = pl.ds(pl.multiple_of(hid * 64, 64), 64)
    square_tmp[...] = jnp.zeros_like(square_tmp)
    for fetch in fetches[:5]:
        fetch.wait()
    square_tmp[0:64, 0:channels] = first_f[...]
    w[own_rows, 0:128] = square_tmp[0:64, :].astype(bf16)
    square_tmp[...] = jnp.zeros_like(square_tmp)
    square_tmp[0:4, 0:64] = hbias_f[...]
    bias[own_rows, :] = square_tmp[...].T[:64]
    for layer, name in enumerate(("g2", "e2", "n2")):
        w[own_rows, COLS[name] : COLS[name] + 256] = gland_a[1, :, 256 * layer : 256 * layer + 256].astype(bf16)
    for fetch in fetches[5:9]:
        fetch.wait()
    for layer, name in enumerate(("e1", "n1", "d1")):
        w[own_rows, COLS[name] : COLS[name] + 512] = gland_a[0, :, 512 * layer : 512 * layer + 512].astype(bf16)
    square_tmp[...] = jnp.zeros_like(square_tmp)
    square_tmp[0:64, 0:channels] = last_f[...]
    w[own_rows, COLS["d2"] : COLS["d2"] + 128] = square_tmp[0:64, :].astype(bf16)
    pl.semaphore_wait(barrier, 3 + row_groups - 1)
    flights = {}
    for name in "gend":
        start, width = GROUPS[name]
        view = functools.partial(rows_of, w, size=64, start=start, width=width)
        flights[name] = gather_start(lambda block, view=view: view(block))
        if name == "g":
            flights["b"] = gather_start(lambda block: rows_of(bias, block, 64))

    def weights_pass(name):
        if name == "b":
            flights[name] = gather_pass(lambda block: rows_of(bias, block, 64), flights[name])
            return
        start, width = GROUPS[name]
        flights[name] = gather_pass(
            lambda block: rows_of(w, block, 64, start, width), flights[name]
        )

    for fetch in fetches[9:]:
        fetch.wait()

    def padded(values, to):
        return jnp.concatenate(
            [values.astype(f32), jnp.zeros((to - channels, values.shape[1]), f32)], 0
        )

    def turn(i, carry):
        at = pl.multiple_of(i * TILE, TILE)
        big[pl.ds(at, TILE), :] = padded(xt[:, pl.ds(at, TILE)], 128).T
        return carry

    lax.fori_loop(0, grid_rows // TILE, turn, 0)
    step_rows = 16
    for block in range(g2m_deg * share // 256):
        k, start = block * 256 // share, block * 256 % share

        def pick(i, carry):
            for u in range(step_rows):
                nacc[block, pl.ds(i * step_rows + u, 1), :] = big[
                    pl.ds(pick_ref[k, hid * share + start + i * step_rows + u], 1), :
                ]
            return carry

        lax.fori_loop(0, 256 // step_rows, pick, 0)

    def unpick(i, carry):
        at = pl.multiple_of(i * TILE, TILE)
        for half in range(2):
            there = pl.ds(pl.multiple_of(at + half * 256, 256), 256)
            dp_d[:PAD, there] = nacc[2 * i + half].T[:PAD].astype(bf16)
        x_ref[:, pl.ds(at, TILE)] = padded(
            xt[:, pl.ds(pl.multiple_of(my_grid + at, TILE), TILE)], PAD
        ).astype(bf16)
        return carry

    lax.fori_loop(0, tiles, unpick, 0)
    square_tmp[...] = jnp.zeros_like(square_tmp)
    for layer in range(3):
        square_tmp[2 * layer : 2 * layer + 2, :] = norm_f[layer][:, :128]
    norm_ref[:128, :] = square_tmp[...].T
    for layer in range(3):
        square_tmp[2 * layer : 2 * layer + 2, :] = norm_f[layer][:, 128:]
    norm_ref[128:, :] = square_tmp[...].T
    square_tmp[...] = jnp.zeros_like(square_tmp)
    square_tmp[0:1, 0:channels] = dbias_f[...]
    square_tmp[1:2, 0:channels] = level_f[...].astype(f32)
    chan_ref[...] = square_tmp[...].T[:PAD]

    for name in "gb":
        weights_pass(name)
    gather_wait(flights["g"])
    gather_wait(flights["b"])
    b_g, b_e, b_n, b_d = (bias[:, k : k + 1] for k in range(4))
    gains = [norm_ref[:, 2 * k : 2 * k + 1] for k in range(3)]
    shifts = [norm_ref[:, 2 * k + 1 : 2 * k + 2] for k in range(3)]
    wt[:, 0:256] = flip(w[:, COLS["g2"] : COLS["g2"] + 256])
    w1g = w[:, 0:128][:, :PAD]

    def embed(inputs):
        pre = mm(w1g, inputs) + b_g
        act, slope = act_forward(pre)
        normed, scale = norm_forward(mm(wt[:, 0:256], act))
        return act, slope, normed, scale

    mesh_tmp[0] = jnp.zeros((latent, share), f32)

    def pool(i, carry):
        here = pl.ds(pl.multiple_of(i * TILE, TILE), TILE)
        mesh_tmp[0] += embed(dp_d[:PAD, here])[2] * gains[0] + shifts[0]
        return carry

    lax.fori_loop(0, g2m_deg, pool, 0)
    h0_mine[...] = mesh_tmp[0] * (1.0 / g2m_deg)
    my_mesh = pl.ds(pl.multiple_of(hid * share, share), share)
    h0_half = h0_mine[...].astype(bf16)
    h0full[:, my_mesh] = h0_half
    node_in[:latent, :] = h0_half
    h0_view = functools.partial(lanes_of, h0full, size=share)
    h0_flight = gather_start(lambda block: h0_view(block))

    lane = lax.broadcasted_iota(jnp.int32, (1, TILE), 1)
    first_row = hid * mine

    def live_mask(i):
        return (first_row + i * TILE + lane < live_ref[0]).astype(f32)

    cacc[...] = jnp.zeros_like(cacc)

    def squares(i, carry):
        here = pl.ds(pl.multiple_of(i * TILE, TILE), TILE)
        delta = (padded(tt[:, here], PAD) - x_ref[:, here].astype(f32)) * live_mask(i)
        cacc[0] += fold(delta * delta)
        return carry

    lax.fori_loop(0, tiles, squares, 0)
    col = lax.broadcasted_iota(jnp.int32, (PAD, 128), 1)
    live_here = jnp.clip(live_ref[0] - first_row, 0, mine).astype(f32)
    square_tmp[...] = jnp.zeros_like(square_tmp)
    square_tmp[:PAD, :] = jnp.where(
        col == 0, jnp.sum(cacc[0], 1, keepdims=True), jnp.where(col == 1, live_here, 0.0)
    )
    small[...] = square_tmp[...].T[:8]
    sum_hid = [
        mail.copy(small, sland_h.at[slot], peer(device))
        for slot, device in enumerate((core, across, corner))
    ]

    def own(i, carry):
        here = pl.ds(pl.multiple_of(i * TILE, TILE), TILE)
        act, slope, normed, scale = embed(x_ref[:, here])
        put(big, 2 * i * 2 * TILE, slope)
        act_g[:, here] = act
        put(big, (2 * i + 1) * 2 * TILE, normed)
        scale_g[:, here] = scale
        dec_in[:latent, here] = (normed * gains[0] + shifts[0]).astype(bf16)
        return carry

    def own_range(a, b):
        lax.fori_loop(a, b, own, 0)

    own_range(0, tiles // 2)
    h0_flight = gather_pass(lambda block: h0_view(block), h0_flight)
    weights_pass("e")
    weights_pass("n")
    weights_pass("d")
    for copy in sum_hid:
        copy.wait()
    small[...] = small[...] + sland_h[0] + sland_h[1] + sland_h[2]
    sum_rows = [
        mail.copy(small, sland_r.at[step - 1], row_peer(lax.rem(row + step, row_groups)))
        for step in range(1, row_groups)
    ]
    own_range(tiles // 2, tiles)
    for name in "end":
        gather_wait(flights[name])
    wt[:, 256:512] = flip(w[:, COLS["e2"] : COLS["e2"] + 256])
    wt[:, 512:768] = flip(w[:, COLS["n2"] : COLS["n2"] + 256])
    wt[:128, 768:1024] = flip(w[:, COLS["d2"] : COLS["d2"] + 128])
    gather_wait(h0_flight)

    e1 = COLS["e1"]
    mesh_tmp[0] = mm(w[:, e1 : e1 + 256], node_in[:latent, :]) + b_e
    mesh_tmp[1] = jnp.zeros((latent, share), f32)

    def edge_index(k):
        return m2m_ref[pl.ds(k, 1), my_mesh]

    def fill(index, base, rows):
        for block, part in enumerate(ones_at(index, base, rows)):
            onehot[block * 256 : block * 256 + 256, :] = part

    def edge(k, carry):
        fill(edge_index(k), 0, mesh_rows)
        sent = mm(h0full[...], onehot[...]).astype(bf16)
        hs_e[k] = sent
        pre = mesh_tmp[0] + mm(w[:, e1 + 256 : e1 + 512], sent)
        act, slope = act_forward(pre)
        act_e[k] = act
        ds_e[k] = slope
        normed, scale = norm_forward(mm(wt[:, 256:512], act))
        nrm_e[k] = normed
        scale_e[pl.ds(k, 1), :] = scale
        mesh_tmp[1] += normed * gains[1] + shifts[1]
        return carry

    lax.fori_loop(0, degree, edge, 0)

    n1 = COLS["n1"]
    node_in[latent:, :] = mesh_tmp[1].astype(bf16)
    act_n, slope_n = act_forward(mm(w[:, n1 : n1 + 512], node_in[...]) + b_n)
    normed_n, scale_n = norm_forward(mm(wt[:, 512:768], act_n))
    h1 = h0_mine[...] + (normed_n * gains[2] + shifts[2])
    ds_e[degree] = slope_n
    act_e[degree] = act_n
    nrm_e[degree] = normed_n
    scale_e[degree : degree + 1, :] = scale_n
    h1full[:, my_mesh] = h1.astype(bf16)
    h1_view = functools.partial(lanes_of, h1full, size=share)
    h1_flight = gather_start(lambda block: h1_view(block))

    for copy in sum_rows:
        copy.wait()
    totals = small[...]
    for step in range(1, row_groups):
        totals = totals + sland_r[step - 1]
    square_tmp[...] = jnp.zeros_like(square_tmp)
    square_tmp[:8, :] = totals
    totals = square_tmp[...].T[:PAD]
    count = totals[:, 1:2]
    var = totals[:, 0:1] / count + 1e-06
    d_bias = chan_ref[:, 0:1]
    level = chan_ref[:, 1:2]
    loss_weight = count * jnp.sum(level, 0, keepdims=True)
    tot_ref[...] = jnp.broadcast_to(loss_weight[:8], (8, 128))
    weight_var = level / var
    pull = 2.0 * weight_var / loss_weight
    nacc[...] = jnp.zeros_like(nacc)
    cacc[...] = jnp.zeros_like(cacc)
    grad[...] = jnp.zeros_like(grad)
    dsum[...] = jnp.zeros_like(dsum)


    def spot(i, write):
        base = my_grid + i * TILE
        for at in range(0, mesh_rows, TILE):
            for block, part in enumerate(ones_at(g2m_ref[:, at : at + TILE], base, TILE)):
                write(block, at, part)

    def spot_store(i, carry):
        def write(block, at, part):
            spots[i, block * 256 : block * 256 + 256, at : at + TILE] = part

        spot(i, write)
        return carry

    ready = spots.shape[0]
    lax.fori_loop(0, ready - 1, spot_store, 0)
    h1_flight = gather_pass(lambda block: h1_view(block), h1_flight)
    lax.fori_loop(ready - 1, ready, spot_store, 0)
    gather_wait(h1_flight)

    def chunk(start, width, block):
        return rows_of(grad, block, 64, start, width)

    def reduce_start(name):
        start, width = GROUPS[name]
        flight = (
            mail.copy(
                chunk(start, width, corner), gland_a.at[1, :, pl.ds(start, width)], peer(core)
            ),
            mail.copy(
                chunk(start, width, core), gland_a.at[0, :, pl.ds(start, width)], peer(core)
            ),
        )
        return flight

    def reduce_across(name, flight):
        start, width = GROUPS[name]
        cols = pl.ds(start, width)
        flight[0].wait()
        view = chunk(start, width, across)
        view[...] = view[...] + gland_a[1, :, cols]
        return flight + (mail.copy(view, gland_b.at[:, cols], peer(across)),)

    def reduce_rows(name, flight):
        start, width = GROUPS[name]
        cols = pl.ds(start, width)
        flight[1].wait()
        flight[2].wait()
        part = 64 // near
        held[:, cols] = chunk(start, width, hid)[...] + gland_a[0, :, cols] + gland_b[:, cols]
        copies = []
        for step in range(1, near):
            to = lax.rem(row_near + step, near)
            copies.append(
                mail.copy(
                    held.at[pl.ds(pl.multiple_of(to * part, part), part), cols],
                    rland.at[step - 1, :, cols],
                    row_peer(row_far * near + to),
                )
            )
        return copies

    def reduce_share(name, copies):
        start, width = GROUPS[name]
        cols = pl.ds(start, width)
        part = 64 // near
        shared = pl.ds(pl.multiple_of(row_near * part, part), part)
        own_part = out_ref.at[shared, cols]
        for copy in copies:
            copy.wait()
        total = held[shared, cols]
        for step in range(1, near):
            total = total + rland[step - 1, :, cols]
        if far > 1:
            own_part[...] = total
            more = []
            for step in range(1, far):
                to = lax.rem(row_far + step, far)
                more.append(
                    mail.copy(
                        own_part,
                        fland.at[step - 1, :, cols],
                        row_peer(to * near + row_near),
                    )
                )
            for copy in more:
                copy.wait()
            for step in range(1, far):
                total = total + fland[step - 1, :, cols]
        own_part[...] = total
        out = []
        for step in range(1, near):
            to = lax.rem(row_near + step, near)
            out.append(mail.copy(own_part, own_part, row_peer(row_far * near + to)))
        return out

    d1, d2 = COLS["d1"], COLS["d2"]
    def decode(i, carry):
        here = pl.ds(pl.multiple_of(i * TILE, TILE), TILE)
        fill(m2g_ref[:, here], 0, mesh_rows)
        back = mm(h1full[...], onehot[...]) * (1.0 / m2g_deg)
        dec_in[latent:, here] = back.astype(bf16)
        pre = mm(w[:, d1 : d1 + 512], dec_in[:, here]) + b_d
        act, slope = act_forward(pre)
        out = mm(wt[:128, 768:1024], act)[:PAD]
        err = x_ref[:, here].astype(f32) + out + d_bias - padded(tt[:, here], PAD)
        kept = err * live_mask(i)
        cacc[1] += fold(weight_var * kept * err)
        pred_grad = pull * kept
        cacc[0] += fold(pred_grad)
        upstream = pred_grad.astype(bf16)
        act_grad = mm(w[:, d2 : d2 + 128][:, :PAD], upstream)
        pre_grad = (act_grad * slope).astype(bf16)
        dp_d[:, here] = pre_grad
        dsum[...] += mt(pre_grad, onehot[...])
        grad[:, d2 : d2 + PAD] += mt(act, upstream)
        return carry

    lax.fori_loop(0, tiles, decode, 0)

    def spread_start(view, land):
        return (
            mail.copy(view(corner), land.at[1], peer(core)),
            mail.copy(view(core), land.at[0], peer(core)),
        )

    def spread_across(view, land, land_far, out, copies):
        copies[0].wait()
        out[...] = (view(across)[...] + land[1]).astype(bf16)
        return copies + (mail.copy(out, land_far, peer(across)),)

    def spread_end(view, land, land_far, copies):
        copies[1].wait()
        copies[2].wait()
        return view(hid)[...] + land[0] + land_far[...].astype(f32)

    d_view = functools.partial(lanes_of, dsum, size=share)

    def view_d(block):
        return d_view(block)

    d_flight = spread_start(view_d, land_a.at[0])
    w1d_low = flip(w[:, d1 : d1 + 256])
    wt[:, 1024:1280] = w1d_low
    d_flight = spread_across(view_d, land_a.at[0], land_b.at[0], half_out, d_flight)

    def decode_rest(i, carry):
        here = pl.ds(pl.multiple_of(i * TILE, TILE), TILE)
        pre_grad = dp_d[:, here]
        grad[:, d1 : d1 + 512] += mt(pre_grad, dec_in[:, here])
        nacc[9] += fold(pre_grad.astype(f32))
        return carry

    lax.fori_loop(0, tiles, decode_rest, 0)
    stage = {"d": reduce_start("d")}
    wt[:, 2304:2560] = flip(w[:, d1 + 256 : d1 + 512])
    wt[:, 1280:1536] = flip(w[:, n1 : n1 + 256])
    wt[:, 1536:1792] = flip(w[:, n1 + 256 : n1 + 512])
    wt[:, 1792:2048] = flip(w[:, e1 : e1 + 256])
    wt[:, 2048:2304] = flip(w[:, e1 + 256 : e1 + 512])

    def write_late(start):
        def write(block, at, part):
            dec_in[block * 256 : block * 256 + 256, start + at : start + at + TILE] = part

        return write

    def write_last(block, at, part):
        (h0full, h1full)[block][:, at : at + TILE] = part

    spot(ready, write_late(0))
    spot(ready + 1, write_late(mesh_rows))
    spot(ready + 2, write_last)

    high, low = split2(spread_end(view_d, land_a.at[0], land_b.at[0], d_flight))
    stage["d"] = reduce_across("d", stage["d"])
    h1_grad = (mm(wt[:, 2304:2560], high) + mm(wt[:, 2304:2560], low)) * (1.0 / m2g_deg)
    nacc[2] += fold(h1_grad * nrm_e[degree])
    nacc[5] += fold(h1_grad)
    up_n = norm_backward(
        h1_grad, nrm_e[degree], scale_e[degree : degree + 1, :], gains[2]
    ).astype(bf16)
    n2 = COLS["n2"]
    pre_grad_n = (mm(w[:, n2 : n2 + 256], up_n) * ds_e[degree]).astype(bf16)
    mesh_tmp[0] = h1_grad + mm(wt[:, 1280:1536], pre_grad_n)
    mesh_tmp[1] = mm(wt[:, 1536:1792], pre_grad_n)

    e2 = COLS["e2"]

    def edge_back(k, carry):
        upstream = mesh_tmp[1]
        normed = nrm_e[k]
        nacc[1] += fold(upstream * normed)
        nacc[4] += fold(upstream)
        up = norm_backward(upstream, normed, scale_e[pl.ds(k, 1), :], gains[1]).astype(bf16)
        pre_grad = (mm(w[:, e2 : e2 + 256], up) * ds_e[k]).astype(bf16)
        mesh_tmp[0] += mm(wt[:, 1792:2048], pre_grad)
        grad[:, e2 : e2 + 256] += mt(act_e[k], up)
        act_e[k] = pre_grad
        nacc[7] += fold(pre_grad.astype(f32))
        return carry

    lax.fori_loop(0, degree, edge_back, 0)

    def senders(block):
        total = None
        for k in range(degree):
            place = k % 4 * TILE
            for half, part in enumerate(ones_at(edge_index(k), block * share, share)):
                onehot[place + half * 256 : place + half * 256 + 256, :] = part
            term = mt(act_e[k], onehot[place : place + TILE, :])
            total = term if total is None else total + term
        view_d(block)[...] = total

    senders(corner)
    e_first = mail.copy(view_d(corner), land_a.at[1, 1], peer(core))
    senders(core)
    e_flight = (e_first, mail.copy(view_d(core), land_a.at[1, 0], peer(core)))
    stage["d"] = reduce_rows("d", stage["d"])
    senders(across)
    e_flight = spread_across(view_d, land_a.at[1], land_b.at[1], half_out, e_flight)
    senders(hid)
    high, low = split2(spread_end(view_d, land_a.at[1], land_b.at[1], e_flight))
    h0_grad = mesh_tmp[0] + mm(wt[:, 2048:2304], high) + mm(wt[:, 2048:2304], low)
    hgfull[:, my_mesh] = (h0_grad * (1.0 / g2m_deg)).astype(bf16)
    hg_view = functools.partial(lanes_of, hgfull, size=share)
    hg_flight = gather_start(lambda block: hg_view(block))

    grad[:, n2 : n2 + 256] = mt(act_e[degree], up_n)
    grad[:, n1 : n1 + 512] = mt(pre_grad_n, node_in[...])
    nacc[8] += fold(pre_grad_n.astype(f32))
    stage["n"] = reduce_start("n")

    def edge_weights(k, carry):
        grad[:, e1 : e1 + 256] += mt(act_e[k], node_in[:latent, :])
        grad[:, e1 + 256 : e1 + 512] += mt(act_e[k], hs_e[k])
        return carry

    lax.fori_loop(0, degree // 2, edge_weights, 0)
    hg_flight = gather_pass(lambda block: hg_view(block), hg_flight)
    stage["n"] = reduce_across("n", stage["n"])
    lax.fori_loop(degree // 2, degree, edge_weights, 0)
    stage["e"] = reduce_start("e")
    stage["d"] = reduce_share("d", stage["d"])
    stage["e"] = reduce_across("e", stage["e"])
    gather_wait(hg_flight)

    def grid_back(i, both):
        here = pl.ds(pl.multiple_of(i * TILE, TILE), TILE)
        upstream = mm(wt[:, 1024:1280], dp_d[:, here]) + both
        normed = take(big, (2 * i + 1) * 2 * TILE)
        nacc[0] += fold(upstream * normed)
        nacc[3] += fold(upstream)
        up = norm_backward(upstream, normed, scale_g[:, here], gains[0]).astype(bf16)
        pre_grad = (mm(w[:, COLS["g2"] : COLS["g2"] + 256], up) * take(big, 2 * i * 2 * TILE)).astype(bf16)
        grad[:, COLS["g2"] : COLS["g2"] + 256] += mt(act_g[:, here], up)
        grad[:, 0:PAD] += mt(pre_grad, x_ref[:, here])
        nacc[6] += fold(pre_grad.astype(f32))

    def grid_ready(i, carry):
        grid_back(i, mt(hgfull[...], spots[i]))
        return carry

    def grid_late(i, carry):
        def write(block, at, part):
            onehot[at + block * 256 : at + block * 256 + 256, :] = part

        spot(i, write)
        both = mt(hgfull[:, 0:TILE], onehot[0:TILE, :])
        for at in range(TILE, mesh_rows, TILE):
            both = both + mt(hgfull[:, at : at + TILE], onehot[at : at + TILE, :])
        grid_back(i, both)
        return carry

    lax.fori_loop(0, ready, grid_ready, 0)
    for name in "ne":
        stage[name] = reduce_rows(name, stage[name])
    for half in range(2):
        grid_back(ready + half, mt(hgfull[...], dec_in[:, half * mesh_rows : (half + 1) * mesh_rows]))
    grid_back(ready + 2, jnp.concatenate([mt(hgfull[...], h0full[...]), mt(hgfull[...], h1full[...])], 1))
    lax.fori_loop(ready + 3, tiles, grid_late, 0)

    block = grad[:, 0:128]
    at_col = lax.broadcasted_iota(jnp.int32, (latent, 128), 1)
    for k in range(4):
        block = jnp.where(at_col == PAD + k, jnp.sum(nacc[6 + k], 1, keepdims=True), block)
    grad[:, 0:128] = block
    stage["g"] = reduce_start("g")
    block = jnp.zeros((latent, 128), f32)
    for k in range(6):
        block = jnp.where(at_col == 2 * (k % 3) + k // 3, jnp.sum(nacc[k], 1, keepdims=True), block)
    norm_ref[...] = block
    block = norm_ref[:PAD, :]
    for k in range(2):
        block = jnp.where(col == 6 + k, jnp.sum(cacc[k], 1, keepdims=True), block)
    norm_ref[:PAD, :] = block
    narrow[...] = norm_ref[...].T[:8]
    narrow_hid = [
        mail.copy(narrow, nland_h.at[slot], peer(device))
        for slot, device in enumerate((core, across, corner))
    ]
    stage["g"] = reduce_across("g", stage["g"])
    for name in "ne":
        stage[name] = reduce_share(name, stage[name])
    for copy in narrow_hid:
        copy.wait()
    narrow[...] = narrow[...] + nland_h[0] + nland_h[1] + nland_h[2]
    narrow_rows = [
        mail.copy(narrow, nland_r.at[step - 1], row_peer(lax.rem(row + step, row_groups)))
        for step in range(1, row_groups)
    ]
    stage["g"] = reduce_rows("g", stage["g"])
    stage["g"] = reduce_share("g", stage["g"])
    for copy in narrow_rows:
        copy.wait()
    total = narrow[...]
    for step in range(1, row_groups):
        total = total + nland_r[step - 1]
    all_ref[...] = total
    for name in "dneg":
        for copy in stage[name]:
            copy.wait()


def adam_step(weight, avg, sq, grad, rate, decay):
    avg_new = 0.5 * avg + 0.5 * grad
    sq_new = 0.5 * sq + 0.5 * grad * grad
    fix = 1.0 - 0.5**STEP_COUNT
    step = avg_new / fix / (jnp.sqrt(sq_new / fix) + 1e-08)
    return (weight - rate * (step + decay * weight), avg_new, sq_new)


def adam_kernel(out_ref, all_ref, tot_ref, *refs):
    ins_hbm, outs_hbm, loss_ref, weight_ref = refs[:21], refs[21:46], refs[46], refs[47]
    ins, outs, turned, sem_in, sem_out = refs[48:69], refs[69:94], refs[94], refs[95], refs[96]
    fetches = [
        pltpu.make_async_copy(source, target, sem_in.at[at])
        for at, (source, target) in enumerate(zip(ins_hbm, ins))
    ]
    for fetch in fetches:
        fetch.start()
    stores = []

    def arrive(array):
        for part in (array, 7 + array, 14 + array):
            fetches[part].wait()

    def leave(array):
        for part in (array, 7 + array, 14 + array) + ((21 + array,) if array < 4 else ()):
            store = pltpu.make_async_copy(outs[part], outs_hbm[part], sem_out.at[part])
            store.start()
            stores.append(store)

    def update(array, at, grad, rate, decay):
        fresh, avg_new, sq_new = adam_step(
            ins[array][at], ins[7 + array][at], ins[14 + array][at], grad, rate, decay
        )
        outs[array][at] = fresh
        outs[7 + array][at] = avg_new
        outs[14 + array][at] = sq_new
        if array < 4:
            outs[21 + array][at] = fresh.astype(bf16)

    everything = (slice(None), slice(None))
    channels = ins[0].shape[1]
    arrive(1)
    for layer, name in enumerate(("e1", "n1", "d1")):
        update(1, (layer,) + everything, out_ref[:, COLS[name] : COLS[name] + 512], 0.05, 0.1)
    leave(1)
    arrive(2)
    for layer, name in enumerate(("g2", "e2", "n2")):
        update(2, (layer,) + everything, out_ref[:, COLS[name] : COLS[name] + 256], 0.05, 0.1)
    leave(2)
    arrive(0)
    update(0, everything, out_ref[:, 0:128][:, :channels], 0.05, 0.1)
    leave(0)
    arrive(3)
    update(3, everything, out_ref[:, COLS["d2"] : COLS["d2"] + 128][:, :channels], 0.05, 0.1)
    leave(3)
    turned[...] = out_ref[:, 0:128].T
    arrive(4)
    update(4, everything, turned[PAD : PAD + 4, :], 0.3, 0.0)
    leave(4)
    arrive(5)
    for layer in range(3):
        update(5, (layer,) + everything, all_ref[2 * layer : 2 * layer + 2, :], 0.3, 0.0)
    leave(5)
    arrive(6)
    update(6, everything, all_ref[6:7, 0:channels], 0.3, 0.0)
    leave(6)
    loss_ref[...] = jnp.sum(all_ref[7:8, 0:PAD], 1, keepdims=True)
    weight_ref[...] = tot_ref[0:1, 0:1]
    for store in stores:
        store.wait()


def body(
    grid_input,
    grid_target,
    live_points,
    level_weight,
    g2m_index,
    m2m_index,
    m2g_index,
    *params,
):
    groups = lax.axis_size("hid")
    row_groups = lax.axis_size("rows")
    masters, avgs, squares = params[:7], params[7:14], params[14:21]
    grid_rows, channels = grid_input.shape
    mesh_rows, degree = m2m_index.shape
    latent = masters[5].shape[2]
    share = mesh_rows // groups
    mine = grid_rows // groups
    g2m_deg = g2m_index.shape[1]
    m2g_deg = m2g_index.shape[1]
    whole = pl.BlockSpec(memory_space=pltpu.VMEM)
    scalar = pl.BlockSpec(memory_space=pltpu.SMEM)
    far_memory = pl.BlockSpec(memory_space=pltpu.HBM)
    g2m = g2m_index.T

    def flat(arrays):
        first, wide, second, last, bias, norm, out_bias = arrays
        return (
            first.T,
            wide.transpose(0, 2, 1),
            second,
            last,
            bias,
            norm.transpose(1, 0, 2),
            out_bias[None],
        )

    operands = flat(masters) + flat(avgs) + flat(squares)
    loads = [
        grid_input.T,
        grid_target.T,
        g2m,
        m2m_index.T,
        m2g_index.T,
        *operands[:7],
        level_weight[None],
    ]
    kept = [jax.ShapeDtypeStruct(v.shape, v.dtype) for v in loads]
    for at in (1, 4):
        kept[at] = jax.ShapeDtypeStruct((kept[at].shape[0], mine), kept[at].dtype)
    copies = count_copies(row_groups)
    near = min(row_groups, 8)
    far = row_groups // near
    summed, spare, totals = pl.pallas_call(
        functools.partial(
            main_kernel, row_groups=row_groups, g2m_deg=g2m_deg, m2g_deg=m2g_deg
        ),
        out_shape=[
            jax.ShapeDtypeStruct((64, PACK), f32),
            jax.ShapeDtypeStruct((8, 256), f32),
            jax.ShapeDtypeStruct((8, 128), f32),
        ],
        in_specs=[scalar] * 2 + [far_memory] * 13,
        out_specs=[whole] * 3,
        scratch_shapes=[pltpu.VMEM(v.shape, v.dtype) for v in kept[:6] + kept[8:]]
        + [
            pltpu.SemaphoreType.DMA((17,)),
            pltpu.VMEM((128, 128), f32),
            pltpu.VMEM((latent, 128), f32),
            pltpu.VMEM((PAD, 128), f32),
            pltpu.VMEM((grid_rows, 128), f32),
            pltpu.VMEM((PAD, mine), bf16),
            pltpu.VMEM((256, PACK), bf16),
            pltpu.VMEM((256, 2560), bf16),
            pltpu.VMEM((256, 128), f32),
            pltpu.VMEM((latent, mesh_rows), bf16),
            pltpu.VMEM((latent, mesh_rows), bf16),
            pltpu.VMEM((latent, mesh_rows), bf16),
            pltpu.VMEM((mesh_rows, TILE), bf16),
            pltpu.VMEM((3, TILE, mesh_rows), bf16),
            pltpu.VMEM((latent, mine), bf16),
            pltpu.VMEM((1, mine), f32),
            pltpu.VMEM((2 * latent, mine), bf16),
            pltpu.VMEM((latent, mine), bf16),
            pltpu.VMEM((degree + 1, latent, share), f32),
            pltpu.VMEM((degree + 1, latent, share), bf16),
            pltpu.VMEM((degree, latent, share), bf16),
            pltpu.VMEM((degree + 1, latent, share), f32),
            pltpu.VMEM((8, share), f32),
            pltpu.VMEM((latent, mesh_rows), f32),
            pltpu.VMEM((2, 2, latent, share), f32),
            pltpu.VMEM((2, latent, share), bf16),
            pltpu.VMEM((latent, share), bf16),
            pltpu.VMEM((256, PACK), f32),
            pltpu.VMEM((2, 64, PACK), f32),
            pltpu.VMEM((64, PACK), f32),
            pltpu.VMEM((64, PACK), f32),
            pltpu.VMEM((near - 1, 64 // near, PACK), f32),
            pltpu.VMEM((max(far - 1, 1), 64 // near, PACK), f32),
            pltpu.VMEM((g2m_deg * share // 256, 256, 128), f32),
            pltpu.VMEM((2, PAD, 128), f32),
            pltpu.VMEM((latent, share), f32),
            pltpu.VMEM((2 * latent, share), bf16),
            pltpu.VMEM((2, latent, share), f32),
            pltpu.VMEM((8, 128), f32),
            pltpu.VMEM((3, 8, 128), f32),
            pltpu.VMEM((row_groups - 1, 8, 128), f32),
            pltpu.VMEM((8, 256), f32),
            pltpu.VMEM((3, 8, 256), f32),
            pltpu.VMEM((row_groups - 1, 8, 256), f32),
            pltpu.SemaphoreType.DMA((copies,)),
            pltpu.SemaphoreType.DMA((copies,)),
        ],
        compiler_params=pltpu.CompilerParams(
            collective_id=0, has_side_effects=True, vmem_limit_bytes=64 * 2**20
        ),
        name="step",
    )(
        live_points,
        g2m,
        *loads,
    )
    shapes = [jax.ShapeDtypeStruct(v.shape, f32) for v in operands]
    shapes += [jax.ShapeDtypeStruct(v.shape, bf16) for v in operands[:4]]
    outs = pl.pallas_call(
        adam_kernel,
        out_shape=shapes + [jax.ShapeDtypeStruct((1, 1), f32)] * 2,
        in_specs=[whole] * 3 + [far_memory] * 21,
        out_specs=[far_memory] * 25 + [whole] * 2,
        scratch_shapes=[pltpu.VMEM(v.shape, v.dtype) for v in operands + tuple(shapes)]
        + [
            pltpu.VMEM((128, 64), f32),
            pltpu.SemaphoreType.DMA((21,)),
            pltpu.SemaphoreType.DMA((25,)),
        ],
        compiler_params=pltpu.CompilerParams(vmem_limit_bytes=64 * 2**20),
        name="adam",
    )(summed, spare, totals, *operands)

    def unflat(arrays):
        first, wide, second, last, bias, norm, out_bias = arrays
        return (
            first.T,
            wide.transpose(0, 2, 1),
            second,
            last,
            bias,
            norm.transpose(1, 0, 2),
            out_bias[0],
        )

    halves = outs[21:25]
    return (
        (outs[25][0, 0], outs[26][0, 0])
        + unflat(outs[0:7])
        + unflat(outs[7:14])
        + unflat(outs[14:21])
        + (halves[0].T, halves[1].transpose(0, 2, 1), halves[2], halves[3])
    )


def solution(mesh):
    weights = (
        P(None, "hid"),
        P(None, None, "hid"),
        P(None, "hid", None),
        P("hid", None),
        P(None, "hid"),
        P(),
        P(),
    )
    in_specs = (
        P("rows", None),
        P("rows", None),
        P("rows"),
        P(),
        P("rows", None),
        P("rows", None),
        P("rows", None),
    ) + weights * 3
    out_specs = (P(), P()) + weights * 3 + weights[:4]
    return jax.shard_map(body, mesh=mesh, in_specs=in_specs, out_specs=out_specs, check_vma=False)
```

time: 259 us -> 161 us (0.62)
  Pallas kernels: 213 us -> 159 us
  local copies, waits for them, and re-layouts: 35.4 us -> 0 us
  other arithmetic: 5.56 us -> 0 us
    pallas_call x1, Pallas kernels: 195 us -> 154 us  [body(): pl.pallas_call(functools.partial(main_kernel, row_groups=row_groups, g2m_...]
    unnamed x70 -> x0, local copies, waits for them, and re-layouts: 27.6 us -> none
    pallas_call x2 -> x1, Pallas kernels: 17.5 us -> 5.35 us  [body(): pl.pallas_call(adam_kernel, out_shape=shapes + [jax.ShapeDtypeStruct((1,...]
    pad x6 -> x0, local copies, waits for them, and re-layouts: 3.89 us -> none  [the longest x3 1.98 us: flat(): jnp.pad(out_bias[None], ((0, 0), (0, 128 - channels)))]
where the time goes in v2:
time: 161 us
  Pallas kernels  159 us (99%)
    pallas_call x1, Pallas kernels, body(): pl.pallas_call(functools.partial(main_kernel, row_groups=row_groups, g2m_...  154 us
    pallas_call x1, Pallas kernels, body(): pl.pallas_call(adam_kernel, out_shape=shapes + [jax.ShapeDtypeStruct((1,...  5.35 us

profile of v2, /device:TPU:0, one launch (start us, length us, event | category | flops | bytes accessed | tf_op | source)
XLA Modules:
  0.0 160.9 jit_solution(394020800813665855)
XLA Ops:
  1.3 154.1 %step.1 = (f32[64,2560]{1,0:T(8,128)}, f32[8,256]{1,0:T(8,128)}, f32[8,128]{1,0:T(8,128)}) custom-call(s32[1]{0:T(128)S(6)} %copy.55.live_ref, s32[8,2048]{1,0:T(8,128)} %bitcast.40, bf16[78,16384]{1,0:T(8,128)(2,1)} %bitcast.34, bf16[78,16384]{1,0:T(8,128)(2,1)} %bitcast.35, s32[8,2048]{1,0:T(8,128)} %bitcast.41, s32[6,2048]{1,0:T(8,128)} %bitcast.45, ...), custom_call_target="tpu_custom_call" | custom-call | tf_op jit(solution)/shard_map/step/pallas_call | solution.py:978
  155.4 5.4 %adam.1 = (f32[64,78]{1,0:T(8,128)}, f32[3,64,512]{2,1,0:T(8,128)}, f32[3,64,256]{2,1,0:T(8,128)}, f32[64,78]{1,0:T(8,128)}, f32[4,64]{1,0:T(4,128)}, /*index=5*...) custom-call(f32[64,2560]{1,0:T(8,128)} %get-tuple-element.57.out_ref, ...), custom_call_target="tpu_custom_call" | custom-call | tf_op jit(solution)/shard_map/adam/pallas_call | solution.py:1049
